TPU v7x, 512 devices: a whole 4x8x8 slice. The times are simulated.
512 devices in a mesh: ulysses: 8 (over y_lo, core), blk: 64 (over z, y_hi, x).
Axes of the slice: x: 4, y: 8 (y_hi: 2, y_lo: 4; y = y_hi * 4 + y_lo), z: 8, core: 2. Of those that a mesh axis runs over, the one named last changes fastest.
Arguments:
- queries: bfloat16 [65536, 4096], P(('ulysses', 'blk')), may hold values from -6 to 6
- keys: bfloat16 [65536, 512], P(('ulysses', 'blk')), may hold values from -6 to 6
- values: bfloat16 [65536, 512], P(('ulysses', 'blk')), may hold values from -6 to 6
- grad_out: bfloat16 [65536, 4096], P(('ulysses', 'blk')), may hold values from -6 to 6
- attn_out: bfloat16 [8, 8192, 4096], P(None, 'blk', 'ulysses'), may hold values from -2 to 2
- log_norm: float32 [8, 32, 8192], P(None, 'ulysses', 'blk'), may hold values from 3 to 5
- doc_start: int32 [8, 8192], P(None, 'blk'), may hold values from 0 to 65535, as said below
Outputs:
- grad_queries: bfloat16 [65536, 4096], P(('ulysses', 'blk'))
- grad_keys: bfloat16 [65536, 512], P(('ulysses', 'blk'))
- grad_values: bfloat16 [65536, 512], P(('ulysses', 'blk'))
Inputs may be any that keep to these rules, and one draw needn't show every extreme that they name: doc_start[t] is the first position of the document that holds position t: it is t itself or equals doc_start of position t - 1, it is 0 at position 0, and the last position begins a document of its own.
All inputs are finite; a program needn't handle non-finite values.
Results may differ from a plain program's by a relative error of at most 0.012.
Values may be sent and summed in bfloat16 or wider, within the bound.
No kernel may reach another device: no remote copies, remote signals or barrier semaphores. Data moves between devices by JAX's collectives and lax.ppermute only.
A program may use at most 64 MiB of HBM per device.

v0:
```python
import jax
import jax.numpy as jnp
from jax import lax
from jax.sharding import PartitionSpec as P

DH = 128


def passed_along(value, axis, steps):
    count = lax.axis_size(axis)
    pairs = [(source, (source + steps) % count) for source in range(count)]
    return lax.ppermute(value, axis, pairs)


def roll_stretches(stretched, amount, active):
    return jnp.where(active, jnp.roll(stretched, amount, axis=0), stretched)


def body(queries, keys, values, grad_out, attn_out, log_norm, doc_start):
    groups = lax.axis_size("ulysses")
    cycle_size = lax.axis_size("blk")
    cycle_place = lax.axis_index("blk")
    tokens_dev = queries.shape[0]
    kv_heads = keys.shape[1] // DH
    slot_count = max(groups, kv_heads)
    copies = slot_count // kv_heads
    local_slots = slot_count // groups
    local_heads = queries.shape[1] // DH // groups
    per_slot = local_heads // local_slots
    window = 3 * tokens_dev // 2
    score_scale = DH ** (-0.5)
    paired = jnp.stack(
        [keys.reshape(tokens_dev, kv_heads, DH), values.reshape(tokens_dev, kv_heads, DH)], axis=2
    )
    paired = jnp.repeat(paired, copies, axis=1).reshape(tokens_dev, slot_count * 2 * DH)
    q_local, g_local, kv_local = (
        lax.all_to_all(queries, "ulysses", split_axis=1, concat_axis=0, tiled=True),
        lax.all_to_all(grad_out, "ulysses", split_axis=1, concat_axis=0, tiled=True),
        lax.all_to_all(paired, "ulysses", split_axis=1, concat_axis=0, tiled=True),
    )
    q_local = q_local.reshape(groups, tokens_dev, local_slots, per_slot, DH)
    g_local = g_local.reshape(groups, tokens_dev, local_slots, per_slot, DH)
    kv_local = kv_local.reshape(groups, tokens_dev, local_slots, 2, DH)
    own_block = (kv_local[:, :, :, 0], kv_local[:, :, :, 1])
    out_local = attn_out.reshape(groups, tokens_dev, local_slots, per_slot, DH)
    row_delta = jnp.sum(g_local.astype(jnp.float32) * out_local.astype(jnp.float32), axis=-1)
    row_delta = jnp.moveaxis(row_delta, 1, -1)
    log_local = log_norm.reshape(groups, local_slots, per_slot, tokens_dev)
    at_start = cycle_place < 1
    at_end = cycle_place == cycle_size - 1
    current = own_block
    arrived = []
    for hop in range(2):
        received = passed_along((current[0], current[1]), "blk", 1)
        current = (
            roll_stretches(received[0], 1, at_start),
            roll_stretches(received[1], 1, at_start),
        )
        arrived.append(current)
    near_block, far_block = arrived
    far_rows = far_block[0].shape[1]
    key_all = jnp.concatenate([far_block[0], near_block[0], own_block[0]], axis=1)
    val_all = jnp.concatenate([far_block[1], near_block[1], own_block[1]], axis=1)
    key_span = far_rows + 2 * tokens_dev
    stretch_batch = min(groups, max(1, 512 // tokens_dev))
    batch_count = groups // stretch_batch
    stretch_base = (jnp.arange(groups, dtype=jnp.int32) * cycle_size + cycle_place) * tokens_dev
    query_rows = jnp.arange(tokens_dev, dtype=jnp.int32)[:, None]
    offsets = jnp.arange(key_span, dtype=jnp.int32)[None, :] - far_rows - tokens_dev

    def regroup(stacked):
        return stacked.reshape((batch_count, stretch_batch) + stacked.shape[1:])

    def tile_grads(pieces):
        q_part, g_part, k_part, v_part, log_part, delta_part, start_part, base_part = pieces
        allowed = (offsets <= query_rows) & (offsets > query_rows - window)
        allowed = allowed[None] & (
            base_part[:, None, None] + offsets[None] >= start_part[:, :, None]
        )
        allowed = allowed[:, None, None]
        scores = (
            jnp.einsum("cqsgd,cksd->csgqk", q_part, k_part, preferred_element_type=jnp.float32)
            * score_scale
        )
        weights = jnp.where(allowed, jnp.exp(scores - log_part[..., None]), 0.0)
        weights_low = weights.astype(jnp.bfloat16)
        grad_val = jnp.einsum(
            "csgqk,cqsgd->cksd", weights_low, g_part, preferred_element_type=jnp.float32
        )
        grad_weights = jnp.einsum(
            "cqsgd,cksd->csgqk", g_part, v_part, preferred_element_type=jnp.float32
        )
        dscore = (weights * (grad_weights - delta_part[..., None])).astype(jnp.bfloat16)
        grad_query = (
            jnp.einsum("csgqk,cksd->cqsgd", dscore, k_part, preferred_element_type=jnp.float32)
            * score_scale
        )
        grad_key = (
            jnp.einsum("csgqk,cqsgd->cksd", dscore, q_part, preferred_element_type=jnp.float32)
            * score_scale
        )
        return (grad_query.astype(jnp.bfloat16), grad_key, grad_val)

    outputs = lax.map(
        tile_grads,
        (
            regroup(q_local),
            regroup(g_local),
            regroup(key_all),
            regroup(val_all),
            regroup(log_local),
            regroup(row_delta),
            regroup(doc_start),
            regroup(stretch_base),
        ),
    )
    grad_query = outputs[0].reshape(groups * tokens_dev, local_heads * DH)
    grad_key = outputs[1].reshape(groups, key_span, local_slots, DH)
    grad_val = outputs[2].reshape(groups, key_span, local_slots, DH)
    travel = (grad_key[:, :far_rows], grad_val[:, :far_rows])
    key_total = grad_key[:, far_rows + tokens_dev :]
    val_total = grad_val[:, far_rows + tokens_dev :]
    for hop in range(2):
        received = passed_along((travel[0], travel[1]), "blk", -1)
        received = (
            roll_stretches(received[0], -1, at_end),
            roll_stretches(received[1], -1, at_end),
        )
        if hop == 0:
            padding = ((0, 0), (tokens_dev - far_rows, 0), (0, 0), (0, 0))
            travel = (
                grad_key[:, far_rows : far_rows + tokens_dev] + received[0],
                grad_val[:, far_rows : far_rows + tokens_dev] + received[1],
            )
        else:
            key_total = key_total + received[0]
            val_total = val_total + received[1]
    grad_queries = lax.all_to_all(grad_query, "ulysses", split_axis=0, concat_axis=1, tiled=True)
    back_key, back_val = (
        lax.all_to_all(
            key_total.reshape(groups * tokens_dev, local_slots * DH).astype(jnp.bfloat16),
            "ulysses",
            split_axis=0,
            concat_axis=1,
            tiled=True,
        ).astype(jnp.float32),
        lax.all_to_all(
            val_total.reshape(groups * tokens_dev, local_slots * DH).astype(jnp.bfloat16),
            "ulysses",
            split_axis=0,
            concat_axis=1,
            tiled=True,
        ).astype(jnp.float32),
    )
    grad_keys = (
        back_key.reshape(tokens_dev, kv_heads, copies, DH)
        .sum(axis=2)
        .reshape(tokens_dev, kv_heads * DH)
    )
    grad_values = (
        back_val.reshape(tokens_dev, kv_heads, copies, DH)
        .sum(axis=2)
        .reshape(tokens_dev, kv_heads * DH)
    )
    return (grad_queries, grad_keys.astype(jnp.bfloat16), grad_values.astype(jnp.bfloat16))


def solution(mesh):
    return jax.shard_map(
        body,
        mesh=mesh,
        in_specs=(
            P(("ulysses", "blk"), None),
            P(("ulysses", "blk"), None),
            P(("ulysses", "blk"), None),
            P(("ulysses", "blk"), None),
            P(None, "blk", "ulysses"),
            P(None, "ulysses", "blk"),
            P(None, "blk"),
        ),
        out_specs=(
            P(("ulysses", "blk"), None),
            P(("ulysses", "blk"), None),
            P(("ulysses", "blk"), None),
        ),
        check_vma=False,
    )
```

profile of v0, /device:TPU:1, one launch (start us, length us, event | category | flops | bytes accessed | tf_op | source)
XLA Modules:
  0.0 301.7 jit_solution(13558552414325647459)
XLA Ops:
  1.6 1.0 stack_reshape.7
  3.9 10.3 %all-to-all-start = ((bf16[128,8,256]{0,2,1:T(8,128)(2,1)}), bf16[128,8,256]{0,2,1:T(8,128)(2,1)S(1)}, u32[]{:S(2)}, u32[]{:S(2)}) async-start(bf16[128,8,256]{0,2,1:T(8,128)(2,1)} %bitcast), calls=%async_computation | async-start | bytes 1048576 | tf_op jit(solution)/shard_map/all_to_all | solution.py:39
  14.2 1.3 copy.75
  15.5 13.2 %all-to-all-done = bf16[128,8,256]{0,2,1:T(8,128)(2,1)S(1)} async-done(((bf16[128,8,256]{0,2,1:T(8,128)(2,1)}), bf16[128,8,256]{0,2,1:T(8,128)(2,1)S(1)}, u32[]{:S(2)}, u32[]{:S(2)}) %all-to-all-start) | async-done | bytes 524320 | tf_op jit(solution)/shard_map/all_to_all | solution.py:39
  28.7 4.3 %all-to-all-start.2 = ((bf16[128,8,512]{0,2,1:T(8,128)(2,1)}), bf16[128,8,512]{0,2,1:T(8,128)(2,1)S(1)}, u32[]{:S(2)}, u32[]{:S(2)}) async-start(bf16[128,8,512]{0,2,1:T(8,128)(2,1)} %bitcast.17), calls=%async_computation.2 | async-start | bytes 2097152 | tf_op jit(solution)/shard_map/all_to_all | solution.py:38
  33.1 1.3 copy.71
  34.3 24.5 %all-to-all-done.2 = bf16[128,8,512]{0,2,1:T(8,128)(2,1)S(1)} async-done(((bf16[128,8,512]{0,2,1:T(8,128)(2,1)}), bf16[128,8,512]{0,2,1:T(8,128)(2,1)S(1)}, u32[]{:S(2)}, u32[]{:S(2)}) %all-to-all-start.2) | async-done | bytes 1048608 | tf_op jit(solution)/shard_map/all_to_all | solution.py:38
  58.8 4.3 %all-to-all-start.1 = ((bf16[128,8,512]{0,2,1:T(8,128)(2,1)}), bf16[128,8,512]{0,2,1:T(8,128)(2,1)S(1)}, u32[]{:S(2)}, u32[]{:S(2)}) async-start(bf16[128,8,512]{0,2,1:T(8,128)(2,1)} %bitcast.8), calls=%async_computation.1 | async-start | bytes 2097152 | tf_op jit(solution)/shard_map/all_to_all | solution.py:37
  63.1 1.1 slice_bitcast_fusion
  64.2 2.0 collective-permute-start.2
  66.3 1.9 collective-permute-start
  68.2 40.8 %collective-permute-done.2 = bf16[8,128,1,128]{1,3,0,2:T(8,128)(2,1)} collective-permute-done((bf16[8,128,1,128]{1,3,0,2:T(8,128)(2,1)}, bf16[8,128,1,128]{1,3,0,2:T(8,128)(2,1)}, u32[]{:S(2)}, u32[]{:S(2)}) %collective-permute-start.2) | collective-permute-done | bytes 262176 | tf_op jit(solution)/shard_map/ppermute | solution.py:12
  111.5 1.9 collective-permute-start.3
  113.4 1.2 collective-permute-done
  115.4 1.9 collective-permute-start.1
  117.4 1.3 copy.76
  118.7 1.1 copy.70
  119.8 1.1 copy.74
  121.0 1.8 copy.73
  122.8 1.8 copy.69
  124.6 11.6 %collective-permute-done.3 = bf16[8,128,1,128]{1,3,0,2:T(8,128)(2,1)} collective-permute-done((bf16[8,128,1,128]{1,3,0,2:T(8,128)(2,1)}, bf16[8,128,1,128]{1,3,0,2:T(8,128)(2,1)}, u32[]{:S(2)}, u32[]{:S(2)}) %collective-permute-start.3) | collective-permute-done | bytes 262176 | tf_op jit(solution)/shard_map/ppermute | solution.py:12
  138.8 3.2 %collective-permute-done.1 = bf16[8,128,1,128]{1,3,0,2:T(8,128)(2,1)} collective-permute-done((bf16[8,128,1,128]{1,3,0,2:T(8,128)(2,1)}, bf16[8,128,1,128]{1,3,0,2:T(8,128)(2,1)}, u32[]{:S(2)}, u32[]{:S(2)}) %collective-permute-start.1) | collective-permute-done | bytes 262176 | tf_op jit(solution)/shard_map/ppermute | solution.py:12
  144.6 2.3 pad_maximum_fusion
  147.6 14.9 %while.18 = (s32[]{:T(128)}, bf16[2,4,128,1,4,128]{2,5,4,1,3,0:T(8,128)(2,1)}, f32[2,4,384,1,128]{2,4,1,3,0:T(8,128)}, f32[2,4,384,1,128]{2,4,1,3,0:T(8,128)}, b...) while((s32[]{:T(128)}, ...), condition=%wide.region_2.3_spmd.clone.clone, body=%wide.region_1.2_spmd.clone.clone.sunk | while | flops 1015760896 | bytes 44421956 | solution.py:104
  149.3 1.0 fusion.111
  152.5 1.0 copy-done.8
  153.4 1.6 fusion.114
  156.7 1.0 fusion.111
  159.9 1.0 copy-done.8
  160.9 1.7 fusion.114
  162.6 1.1 slice.119
  163.6 2.1 collective-permute-start.6
  165.8 1.1 slice.112
  166.9 1.9 collective-permute-start.4
  168.8 43.6 %collective-permute-done.6 = f32[8,128,1,128]{1,3,0,2:T(8,128)S(1)} collective-permute-done((f32[8,128,1,128]{1,3,0,2:T(8,128)S(1)}, f32[8,128,1,128]{1,3,0,2:T(8,128)S(1)}, u32[]{:S(2)}, u32[]{:S(2)}) %collective-permute-start.6) | collective-permute-done | bytes 524320 | tf_op jit(solution)/shard_map/ppermute | solution.py:12
  212.5 1.2 slice_add_fusion
  213.7 12.4 %collective-permute-start.7 = (f32[8,128,1,128]{1,3,0,2:T(8,128)S(1)}, f32[8,128,1,128]{1,3,0,2:T(8,128)S(1)}, u32[]{:S(2)}, u32[]{:S(2)}) collective-permute-start(f32[8,128,1,128]{1,3,0,2:T(8,128)S(1)} %slice_add_fusion), channel_id=1, source_target_pairs={{0,63},{1,0},{2,1},{3,2},{4,3},{5,4},{6,5},{7,6},{8,7},{9,8},{10,9... | collective-permute-start | bytes 1572872 | tf_op jit(solution)/shard_map/ppermute | solution.py:12
  227.1 10.0 %collective-permute-start.5 = (f32[8,128,1,128]{1,3,0,2:T(8,128)}, f32[8,128,1,128]{1,3,0,2:T(8,128)S(1)}, u32[]{:S(2)}, u32[]{:S(2)}) collective-permute-start(f32[8,128,1,128]{1,3,0,2:T(8,128)} %slice_add_fusion.2), channel_id=1, source_target_pairs={{0,63},{1,0},{2,1},{3,2},{4,3},{5,4},{6,5},{7,6},{8,7},{9,8},{10,9... | collective-permute-start | bytes 1572872 | tf_op jit(solution)/shard_map/ppermute | solution.py:12
  237.1 1.8 fusion.78
  238.9 4.5 %all-to-all-start.5 = ((bf16[8,128,128]{1,2,0:T(8,128)(2,1)}), bf16[8,128,128]{1,2,0:T(8,128)(2,1)S(1)}, u32[]{:S(2)}, u32[]{:S(2)}) async-start(bf16[8,128,128]{1,2,0:T(8,128)(2,1)} %fusion.78), calls=%async_computation.5 | async-start | bytes 524288 | tf_op jit(solution)/shard_map/all_to_all | solution.py:147
  243.4 4.8 %collective-permute-done.5 = f32[8,128,1,128]{1,3,0,2:T(8,128)S(1)} collective-permute-done((f32[8,128,1,128]{1,3,0,2:T(8,128)}, f32[8,128,1,128]{1,3,0,2:T(8,128)S(1)}, u32[]{:S(2)}, u32[]{:S(2)}) %collective-permute-start.5) | collective-permute-done | bytes 524320 | tf_op jit(solution)/shard_map/ppermute | solution.py:12
  249.1 6.0 %all-to-all-done.5 = bf16[8,128,128]{1,2,0:T(8,128)(2,1)S(1)} async-done(((bf16[8,128,128]{1,2,0:T(8,128)(2,1)}), bf16[8,128,128]{1,2,0:T(8,128)(2,1)S(1)}, u32[]{:S(2)}, u32[]{:S(2)}) %all-to-all-start.5) | async-done | bytes 262176 | tf_op jit(solution)/shard_map/all_to_all | solution.py:147
  255.1 5.6 %all-to-all-start.4 = ((bf16[8,128,128]{1,2,0:T(8,128)(2,1)}), bf16[8,128,128]{1,2,0:T(8,128)(2,1)S(1)}, u32[]{:S(2)}, u32[]{:S(2)}) async-start(bf16[8,128,128]{1,2,0:T(8,128)(2,1)} %fusion.77), calls=%async_computation.4 | async-start | bytes 524288 | tf_op jit(solution)/shard_map/all_to_all | solution.py:140
  260.7 1.3 copy.94
  262.0 7.4 %all-to-all-done.4 = bf16[8,128,128]{1,2,0:T(8,128)(2,1)S(1)} async-done(((bf16[8,128,128]{1,2,0:T(8,128)(2,1)}), bf16[8,128,128]{1,2,0:T(8,128)(2,1)S(1)}, u32[]{:S(2)}, u32[]{:S(2)}) %all-to-all-start.4) | async-done | bytes 262176 | tf_op jit(solution)/shard_map/all_to_all | solution.py:140
  269.4 4.5 %all-to-all-start.3 = ((bf16[8,128,512]{2,1,0:T(8,128)(2,1)}), bf16[8,128,512]{2,1,0:T(8,128)(2,1)S(1)}, u32[]{:S(2)}, u32[]{:S(2)}) async-start(bf16[8,128,512]{2,1,0:T(8,128)(2,1)} %copy.94), calls=%async_computation.3 | async-start | bytes 2097152 | tf_op jit(solution)/shard_map/all_to_all | solution.py:138
  275.6 24.1 %all-to-all-done.3 = bf16[8,128,512]{2,1,0:T(8,128)(2,1)S(1)} async-done(((bf16[8,128,512]{2,1,0:T(8,128)(2,1)}), bf16[8,128,512]{2,1,0:T(8,128)(2,1)S(1)}, u32[]{:S(2)}, u32[]{:S(2)}) %all-to-all-start.3) | async-done | bytes 1048608 | tf_op jit(solution)/shard_map/all_to_all | solution.py:138
  300.3 1.3 copy.81
  (97 shorter events, 23.0 us)
Async XLA Ops:
  1.6 12.6 %copy-start.4 = (bf16[128,4096]{1,0:T(8,128)(2,1)S(1)}, bf16[128,4096]{1,0:T(8,128)(2,1)}, u32[]{:S(2)}) copy-start(bf16[128,4096]{1,0:T(8,128)(2,1)} %param.12) | copy-start | bytes 3145732
  3.9 24.8 %all-to-all-start = ((bf16[128,8,256]{0,2,1:T(8,128)(2,1)}), bf16[128,8,256]{0,2,1:T(8,128)(2,1)S(1)}, u32[]{:S(2)}, u32[]{:S(2)}) async-start(bf16[128,8,256]{0,2,1:T(8,128)(2,1)} %bitcast), calls=%async_computation | async-start | bytes 1048576 | tf_op jit(solution)/shard_map/all_to_all | solution.py:39
  15.5 17.5 %copy-start.5 = (bf16[128,4096]{1,0:T(8,128)(2,1)S(1)}, bf16[128,4096]{1,0:T(8,128)(2,1)}, u32[]{:S(2)}) copy-start(bf16[128,4096]{1,0:T(8,128)(2,1)} %param.9) | copy-start | bytes 3145732
  28.7 30.1 %all-to-all-start.2 = ((bf16[128,8,512]{0,2,1:T(8,128)(2,1)}), bf16[128,8,512]{0,2,1:T(8,128)(2,1)S(1)}, u32[]{:S(2)}, u32[]{:S(2)}) async-start(bf16[128,8,512]{0,2,1:T(8,128)(2,1)} %bitcast.17), calls=%async_computation.2 | async-start | bytes 2097152 | tf_op jit(solution)/shard_map/all_to_all | solution.py:38
  58.8 88.5 %all-to-all-start.1 = ((bf16[128,8,512]{0,2,1:T(8,128)(2,1)}), bf16[128,8,512]{0,2,1:T(8,128)(2,1)S(1)}, u32[]{:S(2)}, u32[]{:S(2)}) async-start(bf16[128,8,512]{0,2,1:T(8,128)(2,1)} %bitcast.8), calls=%async_computation.1 | async-start | bytes 2097152 | tf_op jit(solution)/shard_map/all_to_all | solution.py:37
  64.2 53.2 %copy-start.6 = (bf16[8,128,512]{2,1,0:T(8,128)(2,1)S(1)}, bf16[8,128,512]{2,1,0:T(8,128)(2,1)}, u32[]{:S(2)}) copy-start(bf16[8,128,512]{2,1,0:T(8,128)(2,1)} %param.13) | copy-start | bytes 3145732
  64.2 44.8 %collective-permute-start.2 = (bf16[8,128,1,128]{1,3,0,2:T(8,128)(2,1)}, bf16[8,128,1,128]{1,3,0,2:T(8,128)(2,1)}, u32[]{:S(2)}, u32[]{:S(2)}) collective-permute-start(bf16[8,128,1,128]{1,3,0,2:T(8,128)(2,1)} %get-tuple-element.311), channel_id=1, source_target_pairs={{0,1},{1,2},{2,3},{3,4},{4,5},{5,6},{6,7},{7,8},{8,9},{9,10},{10,1... | collective-permute-start | bytes 786440 | tf_op jit(solution)/shard_map/ppermute | solution.py:12
  66.3 48.4 %collective-permute-start = (bf16[8,128,1,128]{1,3,0,2:T(8,128)(2,1)}, bf16[8,128,1,128]{1,3,0,2:T(8,128)(2,1)S(1)}, u32[]{:S(2)}, u32[]{:S(2)}) collective-permute-start(bf16[8,128,1,128]{1,3,0,2:T(8,128)(2,1)} %get-tuple-element.312), channel_id=1, source_target_pairs={{0,1},{1,2},{2,3},{3,4},{4,5},{5,6},{6,7},{7,8},{8,9},{9,10},{10,1... | collective-permute-start | bytes 786440 | tf_op jit(solution)/shard_map/ppermute | solution.py:12
  111.5 24.7 %collective-permute-start.3 = (bf16[8,128,1,128]{1,3,0,2:T(8,128)(2,1)}, bf16[8,128,1,128]{1,3,0,2:T(8,128)(2,1)}, u32[]{:S(2)}, u32[]{:S(2)}) collective-permute-start(bf16[8,128,1,128]{1,3,0,2:T(8,128)(2,1)} %maximum_select_fusion.6), channel_id=1, source_target_pairs={{0,1},{1,2},{2,3},{3,4},{4,5},{5,6},{6,7},{7,8},{8,9},{9,10},{10,1... | collective-permute-start | bytes 786440 | tf_op jit(solution)/shard_map/ppermute | solution.py:12
  115.4 26.6 %collective-permute-start.1 = (bf16[8,128,1,128]{1,3,0,2:T(8,128)(2,1)}, bf16[8,128,1,128]{1,3,0,2:T(8,128)(2,1)}, u32[]{:S(2)}, u32[]{:S(2)}) collective-permute-start(bf16[8,128,1,128]{1,3,0,2:T(8,128)(2,1)} %maximum_select_fusion.4), channel_id=1, source_target_pairs={{0,1},{1,2},{2,3},{3,4},{4,5},{5,6},{6,7},{7,8},{8,9},{9,10},{10,1... | collective-permute-start | bytes 786440 | tf_op jit(solution)/shard_map/ppermute | solution.py:12
  144.6 2.3 copy-start
  146.9 0.7 copy-start.11
  146.9 0.7 copy-start.12
  148.2 1.1 copy-start.10
  149.3 1.4 copy-start.1
  150.3 1.3 copy-start.7
  151.3 1.2 copy-start.2
  152.5 1.0 copy-start.8
  155.6 1.1 copy-start.10
  156.7 1.4 copy-start.1
  157.8 1.3 copy-start.7
  158.8 1.2 copy-start.2
  159.9 1.0 copy-start.8
  163.6 48.8 %collective-permute-start.6 = (f32[8,128,1,128]{1,3,0,2:T(8,128)S(1)}, f32[8,128,1,128]{1,3,0,2:T(8,128)S(1)}, u32[]{:S(2)}, u32[]{:S(2)}) collective-permute-start(f32[8,128,1,128]{1,3,0,2:T(8,128)S(1)} %slice.119), channel_id=1, source_target_pairs={{0,63},{1,0},{2,1},{3,2},{4,3},{5,4},{6,5},{7,6},{8,7},{9,8},{10,9... | collective-permute-start | bytes 1572872 | tf_op jit(solution)/shard_map/ppermute | solution.py:12
  166.9 59.3 %collective-permute-start.4 = (f32[8,128,1,128]{1,3,0,2:T(8,128)S(1)}, f32[8,128,1,128]{1,3,0,2:T(8,128)S(1)}, u32[]{:S(2)}, u32[]{:S(2)}) collective-permute-start(f32[8,128,1,128]{1,3,0,2:T(8,128)S(1)} %slice.112), channel_id=1, source_target_pairs={{0,63},{1,0},{2,1},{3,2},{4,3},{5,4},{6,5},{7,6},{8,7},{9,8},{10,9... | collective-permute-start | bytes 1572872 | tf_op jit(solution)/shard_map/ppermute | solution.py:12
  212.5 13.7 %copy-start.3 = (f32[2,4,384,1,128]{2,4,1,3,0:T(8,128)S(1)}, f32[2,4,384,1,128]{2,4,1,3,0:T(8,128)}, u32[]{:S(2)}) copy-start(f32[2,4,384,1,128]{2,4,1,3,0:T(8,128)} %get-tuple-element.182) | copy-start | bytes 4718596
  213.7 23.3 %collective-permute-start.7 = (f32[8,128,1,128]{1,3,0,2:T(8,128)S(1)}, f32[8,128,1,128]{1,3,0,2:T(8,128)S(1)}, u32[]{:S(2)}, u32[]{:S(2)}) collective-permute-start(f32[8,128,1,128]{1,3,0,2:T(8,128)S(1)} %slice_add_fusion), channel_id=1, source_target_pairs={{0,63},{1,0},{2,1},{3,2},{4,3},{5,4},{6,5},{7,6},{8,7},{9,8},{10,9... | collective-permute-start | bytes 1572872 | tf_op jit(solution)/shard_map/ppermute | solution.py:12
  227.1 21.2 %collective-permute-start.5 = (f32[8,128,1,128]{1,3,0,2:T(8,128)}, f32[8,128,1,128]{1,3,0,2:T(8,128)S(1)}, u32[]{:S(2)}, u32[]{:S(2)}) collective-permute-start(f32[8,128,1,128]{1,3,0,2:T(8,128)} %slice_add_fusion.2), channel_id=1, source_target_pairs={{0,63},{1,0},{2,1},{3,2},{4,3},{5,4},{6,5},{7,6},{8,7},{9,8},{10,9... | collective-permute-start | bytes 1572872 | tf_op jit(solution)/shard_map/ppermute | solution.py:12
  238.9 16.2 %all-to-all-start.5 = ((bf16[8,128,128]{1,2,0:T(8,128)(2,1)}), bf16[8,128,128]{1,2,0:T(8,128)(2,1)S(1)}, u32[]{:S(2)}, u32[]{:S(2)}) async-start(bf16[8,128,128]{1,2,0:T(8,128)(2,1)} %fusion.78), calls=%async_computation.5 | async-start | bytes 524288 | tf_op jit(solution)/shard_map/all_to_all | solution.py:147
  243.4 17.3 %copy-start.9 = (bf16[2,4,128,1,4,128]{2,5,4,1,3,0:T(8,128)(2,1)S(1)}, bf16[2,4,128,1,4,128]{2,5,4,1,3,0:T(8,128)(2,1)}, u32[]{:S(2)}) copy-start(bf16[2,4,128,1,4,128]{2,5,4,1,3,0:T(8,128)(2,1)} %get-tuple-element.181) | copy-start | bytes 3145732
  255.1 14.3 %all-to-all-start.4 = ((bf16[8,128,128]{1,2,0:T(8,128)(2,1)}), bf16[8,128,128]{1,2,0:T(8,128)(2,1)S(1)}, u32[]{:S(2)}, u32[]{:S(2)}) async-start(bf16[8,128,128]{1,2,0:T(8,128)(2,1)} %fusion.77), calls=%async_computation.4 | async-start | bytes 524288 | tf_op jit(solution)/shard_map/all_to_all | solution.py:140
  269.4 30.2 %all-to-all-start.3 = ((bf16[8,128,512]{2,1,0:T(8,128)(2,1)}), bf16[8,128,512]{2,1,0:T(8,128)(2,1)S(1)}, u32[]{:S(2)}, u32[]{:S(2)}) async-start(bf16[8,128,512]{2,1,0:T(8,128)(2,1)} %copy.94), calls=%async_computation.3 | async-start | bytes 2097152 | tf_op jit(solution)/shard_map/all_to_all | solution.py:138
where the time goes:
time: 303 us; the launch traced here: 302 us
  waiting for transfers between devices  181 us (60%)
  starting transfers between devices  67.7 us (22%)
  local copies, waits for them, and re-layouts  33.2 us (11%)
  other arithmetic  10.2 us (3%)
  matrix products  8.79 us (3%)
    ppermute x8, waiting for transfers between devices, passed_along(): return lax.ppermute(value, axis, pairs)  105 us
    ppermute x8, starting transfers between devices, passed_along(): return lax.ppermute(value, axis, pairs)  34.2 us
    all_to_all x1, waiting for transfers between devices, body(): lax.all_to_all(grad_out, 'ulysses', split_axis=1, concat_axis=0, tiled=True)  24.5 us
    all_to_all x1, waiting for transfers between devices, body(): lax.all_to_all(grad_query, 'ulysses', split_axis=0, concat_axis=1, tiled=...  24.1 us
    all_to_all x1, waiting for transfers between devices, body(): lax.all_to_all(paired, 'ulysses', split_axis=1, concat_axis=0, tiled=True)  13.2 us
    all_to_all x1, starting transfers between devices, body(): lax.all_to_all(paired, 'ulysses', split_axis=1, concat_axis=0, tiled=True)  10.3 us
    all_to_all x1, waiting for transfers between devices, body(): lax.all_to_all(key_total.reshape(groups * tokens_dev, local_slots * DH).a...  7.4 us
    unnamed x22, local copies, waits for them, and re-layouts  7.09 us
  transfers between devices with their start and end apart: 14, of which 11 were waited for; matrix products, arithmetic and copies ran while one was open for 10% of the time, Pallas kernels for 0%

commit v1 on v0

v1 whole, which is shorter than its diff:
```python
import functools

import jax
import jax.numpy as jnp
from jax import lax
from jax.experimental import pallas as pl
from jax.experimental.pallas import tpu as pltpu
from jax.sharding import PartitionSpec as P

DH = 128
AXES = ("ulysses", "blk")
LOG2E = 1.4426950408889634
BIG = 1e30


def shifted(value, steps):
    count = lax.axis_size("ulysses") * lax.axis_size("blk")
    pairs = [(s, s + steps) for s in range(count) if 0 <= s + steps < count]
    return lax.ppermute(value, AXES, pairs)


def dot(a, b, dims):
    return lax.dot_general(a, b, (dims, ((), ())), preferred_element_type=jnp.float32)


def key_rows(far_ref, near_ref, own_ref):
    return jnp.concatenate([far_ref[...], near_ref[...], own_ref[...]], axis=0)


def mask_bias(base_ref, start_ref, span, tokens):
    far = span - tokens
    key = lax.broadcasted_iota(jnp.int32, (span, tokens), 0) - far
    query = lax.broadcasted_iota(jnp.int32, (span, tokens), 1)
    window = 3 * tokens // 2
    start = start_ref[...] - base_ref[0]
    allowed = (key <= query) & (key > query - window) & (key >= start)
    return jnp.where(allowed, 0.0, -jnp.inf)


def weights_of(keys, q_pair, bias, log_rows):
    scores = dot(keys, q_pair, ((1,), (1,))) * (DH**-0.5 * LOG2E)
    count = len(log_rows)
    shift = jnp.concatenate([bias - LOG2E * row for row in log_rows], axis=1)
    return jnp.exp2(scores + shift)


PAIR = 2


def value_kernel(base_ref, start_ref, q_ref, g_ref, kf_ref, kn_ref, ko_ref, log_ref, far_ref, near_ref, own_ref):
    tokens = q_ref.shape[0]
    heads = q_ref.shape[1] // DH
    keys = key_rows(kf_ref, kn_ref, ko_ref)
    span = keys.shape[0]
    bias = mask_bias(base_ref, start_ref, span, tokens)
    total = None
    for first in range(0, heads, PAIR):
        cut = [slice(h * DH, (h + 1) * DH) for h in range(first, first + PAIR)]
        q_pair = jnp.concatenate([q_ref[:, c] for c in cut], axis=0)
        g_pair = jnp.concatenate([g_ref[:, c] for c in cut], axis=0)
        weights = weights_of(keys, q_pair, bias, [log_ref[h : h + 1, :] for h in range(first, first + PAIR)])
        part = dot(weights.astype(jnp.bfloat16), g_pair, ((1,), (0,)))
        total = part if total is None else total + part
    far = far_ref.shape[0]
    far_ref[...] = total[:far].astype(jnp.bfloat16)
    near_ref[...] = total[far : far + tokens].astype(jnp.bfloat16)
    own_ref[...] = total[far + tokens :]


def key_kernel(base_ref, start_ref, q_ref, g_ref, o_ref, kf_ref, kn_ref, ko_ref, vf_ref, vn_ref, vo_ref, log_ref,
               dq_ref, far_ref, near_ref, own_ref):
    tokens = q_ref.shape[0]
    heads = q_ref.shape[1] // DH
    per = o_ref.shape[2] // DH
    keys = key_rows(kf_ref, kn_ref, ko_ref)
    vals = key_rows(vf_ref, vn_ref, vo_ref)
    span = keys.shape[0]
    vals = jnp.concatenate([vals, jnp.full((span, DH), -1.0, jnp.bfloat16)], axis=1)
    bias = mask_bias(base_ref, start_ref, span, tokens)
    total = None
    for first in range(0, heads, PAIR):
        some = range(first, first + PAIR)
        cut = [slice(h * DH, (h + 1) * DH) for h in some]
        q_pair = jnp.concatenate([q_ref[:, c] for c in cut], axis=0)
        g_pair = jnp.concatenate([g_ref[:, c] for c in cut], axis=0)
        o_pair = jnp.concatenate([o_ref[h // per, :, (h % per) * DH : (h % per + 1) * DH] for h in some], axis=0)
        weights = weights_of(keys, q_pair, bias, [log_ref[h : h + 1, :] for h in some])
        both = jnp.concatenate([g_pair, g_pair * o_pair], axis=1)
        centred = dot(vals, both, ((1,), (1,)))
        dscore = (weights * centred).astype(jnp.bfloat16)
        part = dot(dscore, q_pair, ((1,), (0,)))
        total = part if total is None else total + part
        grad_q = dot(dscore, keys, ((0,), (0,))) * DH**-0.5
        for i, c in enumerate(cut):
            dq_ref[:, c] = grad_q[i * tokens : (i + 1) * tokens].astype(jnp.bfloat16)
    total = total * DH**-0.5
    far = far_ref.shape[0]
    far_ref[...] = total[:far].astype(jnp.bfloat16)
    near_ref[...] = total[far : far + tokens].astype(jnp.bfloat16)
    own_ref[...] = total[far + tokens :]


def body(queries, keys, values, grad_out, attn_out, log_norm, doc_start):
    tokens = queries.shape[0]
    heads = queries.shape[1] // DH
    kv_heads = keys.shape[1] // DH
    group = heads // kv_heads
    ranks = lax.axis_size("ulysses")
    per_rank = group // (heads // ranks)
    far = tokens // 2
    u = lax.axis_index("ulysses")
    place = u * lax.axis_size("blk") + lax.axis_index("blk")
    base = (place * tokens).astype(jnp.int32).reshape(1)
    start = lax.dynamic_slice_in_dim(doc_start, u, 1, 0)

    out_mine = lax.all_to_all(attn_out, "ulysses", split_axis=0, concat_axis=0, tiled=True)
    log_mine = lax.all_to_all(log_norm, "ulysses", split_axis=0, concat_axis=0, tiled=True).reshape(heads, tokens)
    paired = jnp.concatenate([keys, values], axis=1)
    kv_near = shifted(paired, 1)
    kv_far = shifted(paired[tokens - far :], 2)

    smem = pl.BlockSpec(memory_space=pltpu.SMEM)
    whole = lambda shape: pl.BlockSpec(shape, lambda i: (0,) * len(shape))
    cols = lambda rows, width, base=0: pl.BlockSpec((rows, width), lambda i: (0, base + i))
    out_kv = [
        jax.ShapeDtypeStruct((far, kv_heads * DH), jnp.bfloat16),
        jax.ShapeDtypeStruct((tokens, kv_heads * DH), jnp.bfloat16),
        jax.ShapeDtypeStruct((tokens, kv_heads * DH), jnp.float32),
    ]
    out_kv_specs = [cols(far, DH), cols(tokens, DH), cols(tokens, DH)]
    span = 2 * tokens + far
    unit = heads * span * tokens * DH * 2
    params = pltpu.CompilerParams(vmem_limit_bytes=40 * 1024 * 1024)
    log_spec = pl.BlockSpec((group, tokens), lambda i: (i, 0))
    dv_far, dv_near, dv_own = pl.pallas_call(
        value_kernel,
        grid=(kv_heads,),
        in_specs=[smem, whole((1, tokens)), cols(tokens, group * DH), cols(tokens, group * DH),
                  cols(far, DH), cols(tokens, DH), cols(tokens, DH), log_spec],
        out_specs=out_kv_specs,
        out_shape=out_kv,
        compiler_params=params,
        cost_estimate=pl.CostEstimate(flops=4 * unit, bytes_accessed=4 << 20, transcendentals=heads * span * tokens),
        name="value_grads",
    )(base, start, queries, grad_out, kv_far, kv_near, keys, log_mine)
    rv_near = shifted(dv_near, -1)
    rv_far = shifted(dv_far, -2)
    dq, dk_far, dk_near, dk_own = pl.pallas_call(
        key_kernel,
        grid=(kv_heads,),
        in_specs=[smem, whole((1, tokens)), cols(tokens, group * DH), cols(tokens, group * DH),
                  pl.BlockSpec((per_rank, tokens, heads // ranks * DH), lambda i: (i, 0, 0)),
                  cols(far, DH), cols(tokens, DH), cols(tokens, DH),
                  cols(far, DH, kv_heads), cols(tokens, DH, kv_heads), cols(tokens, DH), log_spec],
        out_specs=[cols(tokens, group * DH)] + out_kv_specs,
        out_shape=[jax.ShapeDtypeStruct(queries.shape, jnp.bfloat16)] + out_kv,
        compiler_params=params,
        cost_estimate=pl.CostEstimate(flops=6 * unit, bytes_accessed=6 << 20, transcendentals=heads * span * tokens),
        name="key_grads",
    )(base, start, queries, grad_out, out_mine, kv_far, kv_near, keys, kv_far, kv_near, values, log_mine)
    rk_near = shifted(dk_near, -1)
    rk_far = shifted(dk_far, -2)

    def total(own, near, beyond):
        beyond = jnp.pad(beyond.astype(jnp.float32), ((tokens - far, 0), (0, 0)))
        return (own + near.astype(jnp.float32) + beyond).astype(jnp.bfloat16)

    return dq, total(dk_own, rk_near, rk_far), total(dv_own, rv_near, rv_far)


def solution(mesh):
    return jax.shard_map(
        body,
        mesh=mesh,
        in_specs=(
            P(("ulysses", "blk"), None),
            P(("ulysses", "blk"), None),
            P(("ulysses", "blk"), None),
            P(("ulysses", "blk"), None),
            P(None, "blk", "ulysses"),
            P(None, "ulysses", "blk"),
            P(None, "blk"),
        ),
        out_specs=(
            P(("ulysses", "blk"), None),
            P(("ulysses", "blk"), None),
            P(("ulysses", "blk"), None),
        ),
        check_vma=False,
    )
```

time: 303 us -> 103 us (0.34)
  the two profiles are of different devices: /device:TPU:1 before, /device:TPU:30 now
where the time goes in v1:
time: 103 us
  starting transfers between devices  45.6 us (44%)
  waiting for transfers between devices  33.5 us (33%)
  Pallas kernels  10.6 us (10%)
  blocking collectives  7.5 us (7%)
  local copies, waits for them, and re-layouts  3.39 us (3%)
  other arithmetic  1.39 us (1%)
    ppermute x6, starting transfers between devices, shifted(): return lax.ppermute(value, AXES, pairs)  38.7 us
    ppermute x6, waiting for transfers between devices, shifted(): return lax.ppermute(value, AXES, pairs)  33.5 us
    all_to_all x1, blocking collectives, body(): lax.all_to_all(log_norm, 'ulysses', split_axis=0, concat_axis=0, tiled=True)  7.5 us
    pallas_call x1, Pallas kernels, body(): pl.pallas_call(key_kernel, grid=(kv_heads,), in_specs=[smem, whole((1, to...  7.41 us
    all_to_all x1, starting transfers between devices, body(): lax.all_to_all(attn_out, 'ulysses', split_axis=0, concat_axis=0, tiled=True)  6.89 us
    unnamed x13, local copies, waits for them, and re-layouts  3.36 us
    pallas_call x1, Pallas kernels, body(): pl.pallas_call(value_kernel, grid=(kv_heads,), in_specs=[smem, whole((1,...  3.17 us
  transfers between devices with their start and end apart: 7, of which 3 were waited for; matrix products, arithmetic and copies ran while one was open for 1% of the time, Pallas kernels for 10%

profile of v1, /device:TPU:30, one launch (start us, length us, event | category | flops | bytes accessed | tf_op | source)
XLA Modules:
  0.0 102.7 jit_solution(17596596662000612171)
XLA Ops:
  0.6 0.0 copy-start
  0.6 7.5 %all_to_all.10 = f32[8,4,128]{2,1,0:T(4,128)S(1)} all-to-all(f32[8,4,128]{2,1,0:T(4,128)} %param.12), channel_id=1, replica_groups=mesh['ulysses'=8,'blk'=64] {'ulysses'}, dimensions={0} | all-to-all | bytes 32768 | tf_op jit(solution)/shard_map/all_to_all | solution.py:117
  8.1 0.0 copy-start.1
  8.1 0.0 copy-start.3
  8.2 6.9 %all-to-all-start = ((bf16[8,128,512]{2,1,0:T(8,128)(2,1)}), bf16[8,128,512]{2,1,0:T(8,128)(2,1)S(1)}, u32[]{:S(2)}, u32[]{:S(2)}) async-start(bf16[8,128,512]{2,1,0:T(8,128)(2,1)} %param.11), calls=%async_computation | async-start | bytes 2097152 | tf_op jit(solution)/shard_map/all_to_all | solution.py:116
  15.0 0.0 copy-done.1
  15.0 0.0 copy-start.2
  15.1 0.9 copy-done.2
  16.0 6.0 %collective-permute-start.1 = (bf16[128,1024]{1,0:T(8,128)(2,1)S(1)}, bf16[128,1024]{1,0:T(8,128)(2,1)S(1)}, u32[]{:S(2)}, u32[]{:S(2)}) collective-permute-start(bf16[128,1024]{1,0:T(8,128)(2,1)S(1)} %constant_dynamic-update-slice_fusion), channel_id=1, source_target_pairs={{0,1},{1,2},{2,3},{3,4},{4,5},{5,6},{6,7},{7,8},{8,9},{9,10},{10,1... | collective-permute-start | bytes 786440 | tf_op jit(solution)/shard_map/ppermute | solution.py:19
  22.0 4.3 %collective-permute-start = (bf16[64,1024]{1,0:T(8,128)(2,1)S(1)}, bf16[64,1024]{1,0:T(8,128)(2,1)S(1)}, u32[]{:S(2)}, u32[]{:S(2)}) collective-permute-start(bf16[64,1024]{1,0:T(8,128)(2,1)S(1)} %slice.4), channel_id=1, source_target_pairs={{0,2},{1,3},{2,4},{3,5},{4,6},{5,7},{6,8},{7,9},{8,10},{9,11},{10,... | collective-permute-start | bytes 393224 | tf_op jit(solution)/shard_map/ppermute | solution.py:19
  26.3 0.0 copy-done
  26.4 23.6 %collective-permute-done.kf_ref.vf_ref = bf16[64,1024]{1,0:T(8,128)(2,1)S(1)} collective-permute-done((bf16[64,1024]{1,0:T(8,128)(2,1)S(1)}, bf16[64,1024]{1,0:T(8,128)(2,1)S(1)}, u32[]{:S(2)}, u32[]{:S(2)}) %collective-permute-start) | collective-permute-done | bytes 131104 | tf_op jit(solution)/shard_map/ppermute | solution.py:19
  50.0 0.0 collective-permute-done.1.kn_ref.vn_ref
  50.0 0.0 copy-done.3
  50.0 0.0 copy-start.4
  50.0 1.2 %copy-done.4 = bf16[128,4096]{1,0:T(8,128)(2,1)S(1)} copy-done((bf16[128,4096]{1,0:T(8,128)(2,1)S(1)}, bf16[128,4096]{1,0:T(8,128)(2,1)}, u32[]{:S(2)}) %copy-start.4) | copy-done | bytes 1048600
  51.2 3.2 %value_grads.1 = (bf16[64,512]{1,0:T(8,128)(2,1)S(1)}, bf16[128,512]{1,0:T(8,128)(2,1)S(1)}, f32[128,512]{1,0:T(8,128)S(1)}) custom-call(s32[1]{0:T(128)} %bitcast.base_ref, s32[1,128]{1,0:T(1,128)S(1)} %constant_dynamic-slice_fusion.start_ref, bf16[128,4096]{1,0:T(8,128)(2,1)S(1)} %copy-done.3, bf16[128,4096]{1,0:T(8,128)(2,1)S(1)} %copy-done.4, ...), custom_call_target="tpu_custom_call" | custom-call | flops 1342177280 | bytes 4194304 | tf_op jit(solution)/shard_map/value_grads/pallas_call | solution.py:135
  54.4 22.2 %collective-permute-start.5 = (bf16[64,512]{1,0:T(8,128)(2,1)S(1)}, bf16[64,512]{1,0:T(8,128)(2,1)S(1)}, u32[]{:S(2)}, u32[]{:S(2)}) collective-permute-start(bf16[64,512]{1,0:T(8,128)(2,1)S(1)} %get-tuple-element.16), channel_id=1, source_target_pairs={{2,0},{3,1},{4,2},{5,3},{6,4},{7,5},{8,6},{9,7},{10,8},{11,9},{12,... | collective-permute-start | bytes 196616 | tf_op jit(solution)/shard_map/ppermute | solution.py:19
  76.6 1.9 %collective-permute-start.4 = (bf16[128,512]{1,0:T(8,128)(2,1)S(1)}, bf16[128,512]{1,0:T(8,128)(2,1)S(1)}, u32[]{:S(2)}, u32[]{:S(2)}) collective-permute-start(bf16[128,512]{1,0:T(8,128)(2,1)S(1)} %get-tuple-element.15), channel_id=1, source_target_pairs={{1,0},{2,1},{3,2},{4,3},{5,4},{6,5},{7,6},{8,7},{9,8},{10,9},{11,1... | collective-permute-start | bytes 393224 | tf_op jit(solution)/shard_map/ppermute | solution.py:19
  78.5 0.0 all-to-all-done.o_ref
  78.6 0.0 copy-start.5
  78.6 1.2 %copy-done.5 = bf16[128,4096]{1,0:T(8,128)(2,1)S(1)} copy-done((bf16[128,4096]{1,0:T(8,128)(2,1)S(1)}, bf16[128,4096]{1,0:T(8,128)(2,1)}, u32[]{:S(2)}) %copy-start.5) | copy-done | bytes 1048600
  79.8 7.4 %key_grads.1 = (bf16[128,4096]{1,0:T(8,128)(2,1)}, bf16[64,512]{1,0:T(8,128)(2,1)S(1)}, bf16[128,512]{1,0:T(8,128)(2,1)S(1)}, f32[128,512]{1,0:T(8,128)S(1)}) custom-call(s32[1]{0:T(128)} %bitcast.base_ref, s32[1,128]{1,0:T(1,128)S(1)} %constant_dynamic-slice_fusion.start_ref, bf16[128,4096]{1,0:T(8,128)(2,1)S(1)} %copy-done.3, ...), custom_call_target="tpu_custom_call" | custom-call | flops 2013265920 | bytes 6291456 | tf_op jit(solution)/shard_map/key_grads/pallas_call | solution.py:148
  87.2 1.9 %collective-permute-start.3 = (bf16[64,512]{1,0:T(8,128)(2,1)S(1)}, bf16[64,512]{1,0:T(8,128)(2,1)S(1)}, u32[]{:S(2)}, u32[]{:S(2)}) collective-permute-start(bf16[64,512]{1,0:T(8,128)(2,1)S(1)} %get-tuple-element.13), channel_id=1, source_target_pairs={{2,0},{3,1},{4,2},{5,3},{6,4},{7,5},{8,6},{9,7},{10,8},{11,9},{12,... | collective-permute-start | bytes 196616 | tf_op jit(solution)/shard_map/ppermute | solution.py:19
  89.1 2.3 %collective-permute-start.2 = (bf16[128,512]{1,0:T(8,128)(2,1)S(1)}, bf16[128,512]{1,0:T(8,128)(2,1)S(1)}, u32[]{:S(2)}, u32[]{:S(2)}) collective-permute-start(bf16[128,512]{1,0:T(8,128)(2,1)S(1)} %get-tuple-element.12), channel_id=1, source_target_pairs={{1,0},{2,1},{3,2},{4,3},{5,4},{6,5},{7,6},{8,7},{9,8},{10,9},{11,1... | collective-permute-start | bytes 393224 | tf_op jit(solution)/shard_map/ppermute | solution.py:19
  91.4 0.0 collective-permute-done.5
  91.4 0.0 collective-permute-done.4
  91.4 0.7 add_convert_fusion
  92.1 7.5 %collective-permute-done.3 = bf16[64,512]{1,0:T(8,128)(2,1)S(1)} collective-permute-done((bf16[64,512]{1,0:T(8,128)(2,1)S(1)}, bf16[64,512]{1,0:T(8,128)(2,1)S(1)}, u32[]{:S(2)}, u32[]{:S(2)}) %collective-permute-start.3) | collective-permute-done | bytes 65568 | tf_op jit(solution)/shard_map/ppermute | solution.py:19
  99.7 2.3 %collective-permute-done.2 = bf16[128,512]{1,0:T(8,128)(2,1)S(1)} collective-permute-done((bf16[128,512]{1,0:T(8,128)(2,1)S(1)}, bf16[128,512]{1,0:T(8,128)(2,1)S(1)}, u32[]{:S(2)}, u32[]{:S(2)}) %collective-permute-start.2) | collective-permute-done | bytes 131104 | tf_op jit(solution)/shard_map/ppermute | solution.py:19
  102.0 0.7 add_convert_fusion.1
  (4 shorter events, 0.0 us)
Async XLA Ops:
  0.6 25.7 %copy-start = (s32[8,128]{1,0:T(8,128)S(1)}, s32[8,128]{1,0:T(8,128)}, u32[]{:S(2)}) copy-start(s32[8,128]{1,0:T(8,128)} %param.13) | copy-start | bytes 12292
  8.1 6.9 %copy-start.1 = (bf16[128,512]{1,0:T(8,128)(2,1)S(1)}, bf16[128,512]{1,0:T(8,128)(2,1)}, u32[]{:S(2)}) copy-start(bf16[128,512]{1,0:T(8,128)(2,1)} %ko_ref.3) | copy-start | bytes 393220
  8.1 41.9 %copy-start.3 = (bf16[128,4096]{1,0:T(8,128)(2,1)S(1)}, bf16[128,4096]{1,0:T(8,128)(2,1)}, u32[]{:S(2)}) copy-start(bf16[128,4096]{1,0:T(8,128)(2,1)} %q_ref.3) | copy-start | bytes 3145732
  8.2 70.4 %all-to-all-start = ((bf16[8,128,512]{2,1,0:T(8,128)(2,1)}), bf16[8,128,512]{2,1,0:T(8,128)(2,1)S(1)}, u32[]{:S(2)}, u32[]{:S(2)}) async-start(bf16[8,128,512]{2,1,0:T(8,128)(2,1)} %param.11), calls=%async_computation | async-start | bytes 2097152 | tf_op jit(solution)/shard_map/all_to_all | solution.py:116
  15.0 0.9 copy-start.2
  16.0 34.1 %collective-permute-start.1 = (bf16[128,1024]{1,0:T(8,128)(2,1)S(1)}, bf16[128,1024]{1,0:T(8,128)(2,1)S(1)}, u32[]{:S(2)}, u32[]{:S(2)}) collective-permute-start(bf16[128,1024]{1,0:T(8,128)(2,1)S(1)} %constant_dynamic-update-slice_fusion), channel_id=1, source_target_pairs={{0,1},{1,2},{2,3},{3,4},{4,5},{5,6},{6,7},{7,8},{8,9},{9,10},{10,1... | collective-permute-start | bytes 786440 | tf_op jit(solution)/shard_map/ppermute | solution.py:19
  22.0 28.0 %collective-permute-start = (bf16[64,1024]{1,0:T(8,128)(2,1)S(1)}, bf16[64,1024]{1,0:T(8,128)(2,1)S(1)}, u32[]{:S(2)}, u32[]{:S(2)}) collective-permute-start(bf16[64,1024]{1,0:T(8,128)(2,1)S(1)} %slice.4), channel_id=1, source_target_pairs={{0,2},{1,3},{2,4},{3,5},{4,6},{5,7},{6,8},{7,9},{8,10},{9,11},{10,... | collective-permute-start | bytes 393224 | tf_op jit(solution)/shard_map/ppermute | solution.py:19
  50.0 1.2 %copy-start.4 = (bf16[128,4096]{1,0:T(8,128)(2,1)S(1)}, bf16[128,4096]{1,0:T(8,128)(2,1)}, u32[]{:S(2)}) copy-start(bf16[128,4096]{1,0:T(8,128)(2,1)} %g_ref.3) | copy-start | bytes 3145732
  54.4 37.0 %collective-permute-start.5 = (bf16[64,512]{1,0:T(8,128)(2,1)S(1)}, bf16[64,512]{1,0:T(8,128)(2,1)S(1)}, u32[]{:S(2)}, u32[]{:S(2)}) collective-permute-start(bf16[64,512]{1,0:T(8,128)(2,1)S(1)} %get-tuple-element.16), channel_id=1, source_target_pairs={{2,0},{3,1},{4,2},{5,3},{6,4},{7,5},{8,6},{9,7},{10,8},{11,9},{12,... | collective-permute-start | bytes 196616 | tf_op jit(solution)/shard_map/ppermute | solution.py:19
  76.6 14.8 %collective-permute-start.4 = (bf16[128,512]{1,0:T(8,128)(2,1)S(1)}, bf16[128,512]{1,0:T(8,128)(2,1)S(1)}, u32[]{:S(2)}, u32[]{:S(2)}) collective-permute-start(bf16[128,512]{1,0:T(8,128)(2,1)S(1)} %get-tuple-element.15), channel_id=1, source_target_pairs={{1,0},{2,1},{3,2},{4,3},{5,4},{6,5},{7,6},{8,7},{9,8},{10,9},{11,1... | collective-permute-start | bytes 393224 | tf_op jit(solution)/shard_map/ppermute | solution.py:19
  78.6 1.2 %copy-start.5 = (bf16[128,4096]{1,0:T(8,128)(2,1)S(1)}, bf16[128,4096]{1,0:T(8,128)(2,1)}, u32[]{:S(2)}) copy-start(bf16[128,4096]{1,0:T(8,128)(2,1)} %g_ref.3) | copy-start | bytes 3145732
  87.2 12.5 %collective-permute-start.3 = (bf16[64,512]{1,0:T(8,128)(2,1)S(1)}, bf16[64,512]{1,0:T(8,128)(2,1)S(1)}, u32[]{:S(2)}, u32[]{:S(2)}) collective-permute-start(bf16[64,512]{1,0:T(8,128)(2,1)S(1)} %get-tuple-element.13), channel_id=1, source_target_pairs={{2,0},{3,1},{4,2},{5,3},{6,4},{7,5},{8,6},{9,7},{10,8},{11,9},{12,... | collective-permute-start | bytes 196616 | tf_op jit(solution)/shard_map/ppermute | solution.py:19
  89.1 12.9 %collective-permute-start.2 = (bf16[128,512]{1,0:T(8,128)(2,1)S(1)}, bf16[128,512]{1,0:T(8,128)(2,1)S(1)}, u32[]{:S(2)}, u32[]{:S(2)}) collective-permute-start(bf16[128,512]{1,0:T(8,128)(2,1)S(1)} %get-tuple-element.12), channel_id=1, source_target_pairs={{1,0},{2,1},{3,2},{4,3},{5,4},{6,5},{7,6},{8,7},{9,8},{10,9},{11,1... | collective-permute-start | bytes 393224 | tf_op jit(solution)/shard_map/ppermute | solution.py:19

commit v2 on v1

v2 whole, which is shorter than its diff:
```python
import jax
import jax.numpy as jnp
from jax import lax
from jax.experimental import pallas as pl
from jax.experimental.pallas import tpu as pltpu
from jax.sharding import PartitionSpec as P

DH = 128
AXES = ("ulysses", "blk")
LOG2E = 1.4426950408889634
SCALE = DH**-0.5
RUN = 4
PAD = 16


def shifted(value, steps):
    count = lax.axis_size("ulysses") * lax.axis_size("blk")
    pairs = [(s, s + steps) for s in range(count) if 0 <= s + steps < count]
    return lax.ppermute(value, AXES, pairs)


def routes(steps):
    ranks, blocks = lax.axis_size("ulysses"), lax.axis_size("blk")
    run = min(4, blocks)
    direct, across = [], []
    for source in range(ranks * blocks - steps):
        target = source + steps
        rank, place = divmod(source, blocks)
        if target == (ranks - 2) * blocks:
            direct.append((source, 0))
            across.append((0, target))
        elif place % run + steps == run + steps - 1 and (steps > 1 or target // blocks % 2 == 1):
            middle = (rank if steps > 1 else rank | 1) * blocks + place - run + steps
            direct.append((source, middle))
            across.append((middle, target))
        else:
            direct.append((source, target))
    return direct, across


def passed_on(value, steps):
    direct, across = routes(steps)
    arrived = lax.ppermute(value, AXES, direct)
    return arrived, lax.ppermute(arrived, AXES, across)


def dot(a, b, dims):
    return lax.dot_general(a, b, (dims, ((), ())), preferred_element_type=jnp.float32)


def pair_kernel(k_ref, v_ref, near_ref, far_ref):
    tokens = k_ref.shape[0]
    half = tokens // 2
    near_ref[:tokens] = k_ref[...]
    near_ref[tokens:] = v_ref[...]
    far_ref[:half] = k_ref[half:]
    far_ref[half:] = v_ref[half:]


def pack_kernel(o_ref, log_ref, packed_ref):
    tokens = o_ref.shape[1]
    half = tokens // 2
    packed_ref[:, :tokens] = o_ref[...]
    lane = lax.broadcasted_iota(jnp.int32, (1, tokens), 1)
    for c in range(log_ref.shape[0]):
        rows = []
        for a in range(0, log_ref.shape[1], 2):
            one, two = log_ref[c, a : a + 1, :], log_ref[c, a + 1 : a + 2, :]
            rows.append(jnp.where(lane < half, one, pltpu.roll(two, half, 1)))
            rows.append(jnp.where(lane < half, pltpu.roll(one, half, 1), two))
        left = jnp.concatenate(rows, axis=1)
        terms = []
        for _ in range(3):
            term = left.astype(jnp.bfloat16).astype(jnp.float32)
            left = left - term
            terms.append(term)
        terms.append(jnp.zeros((PAD - 3, left.shape[1]), jnp.float32))
        packed_ref[c, tokens:] = jnp.concatenate(terms, axis=0).astype(jnp.bfloat16)


def head_cols(ref, rows, head):
    return ref[rows, head * DH : (head + 1) * DH]


def stacked_heads(ref, rows, heads):
    return jnp.concatenate([head_cols(ref, rows, h) for h in heads], axis=0)


def out_rows(ref, rows, heads, per):
    return jnp.concatenate([ref[h // per, rows, h % per * DH : (h % per + 1) * DH] for h in heads], axis=0)


def mask_bias(place_ref, start_ref, first_key, first_query, span, half):
    tokens = 2 * half
    key = lax.broadcasted_iota(jnp.int32, (span, tokens), 0) + first_key
    lane = lax.broadcasted_iota(jnp.int32, (span, tokens), 1)
    query = lax.rem(lane, half) + first_query
    start = start_ref[...] - place_ref[0]
    low = lax.broadcasted_iota(jnp.int32, start.shape, 1) < half
    moved = pltpu.roll(start, half, 1)
    start = jnp.where(low, moved, start) if first_query else jnp.where(low, start, moved)
    allowed = (key <= query) & (key > query - 3 * tokens // 2) & (key >= start)
    return jnp.where(allowed, 0.0, -jnp.inf)


def weights_of(keys, q_rows, bias, rows):
    shift = jnp.concatenate([bias - row for row in rows], axis=1)
    return jnp.exp2(dot(keys, q_rows, ((1,), (1,))) * (SCALE * LOG2E) + shift)


def centre_cols(g_rows, o_rows):
    prod = g_rows.astype(jnp.float32) * o_rows.astype(jnp.float32)
    prod = prod + pltpu.roll(prod, DH // 2, 1)
    head = prod.astype(jnp.bfloat16).astype(jnp.float32)
    lane = lax.broadcasted_iota(jnp.int32, prod.shape, 1)
    return jnp.where(lane < DH // 2, head, prod - head).astype(jnp.bfloat16)


def score_grads(weights, vals, g_rows, o_rows):
    vals = jnp.concatenate([vals, jnp.full(vals.shape, -1.0, vals.dtype)], axis=1)
    both = jnp.concatenate([g_rows, centre_cols(g_rows, o_rows)], axis=1)
    return (weights * dot(vals, both, ((1,), (1,)))).astype(jnp.bfloat16)


def key_value_kernel(place_ref, start_ref, q_ref, g_ref, k_own, v_own, far_hbm, far_fixed, near_hbm, near_fixed, packed_hbm,
                     far_out, near_out, dk_own, dv_own, ds_ref, keys_out, far_ref, near_ref, packed_ref, sems):
    tokens, width = q_ref.shape
    half = tokens // 2
    kv_heads = k_own.shape[1] // DH
    group = width // DH // kv_heads
    ranks = packed_ref.shape[0]
    per = width // DH // ranks
    sources = ((far_hbm, far_fixed, far_ref), (near_hbm, near_fixed, near_ref))
    for i, (direct, fixed, target) in enumerate(sources):
        staged = place_ref[1 + i] == 1
        pl.when(staged)(pltpu.make_async_copy(fixed, target, sems.at[i]).start)
        pl.when(jnp.logical_not(staged))(pltpu.make_async_copy(direct, target, sems.at[i]).start)
    moves = []
    for kv in range(kv_heads):
        some = pl.ds(kv * group // per, group // per)
        moves.append((packed_hbm.at[some], packed_ref.at[some]))
    copies = [pltpu.make_async_copy(a, b, sems.at[2 + i]) for i, (a, b) in enumerate(moves)]
    for copy in copies:
        copy.start()
    bias_top = mask_bias(place_ref, start_ref, -3 * half, 0, 4 * half, half)
    bias_low = mask_bias(place_ref, start_ref, -2 * half, half, 4 * half, half)
    top, low = slice(0, half), slice(half, tokens)
    for i, (direct, _, target) in enumerate(sources):
        pltpu.make_async_copy(direct, target, sems.at[i]).wait()
    keys_out[:half] = far_ref[:half]
    keys_out[half:] = near_ref[:tokens]
    for kv in range(kv_heads):
        copies[kv].wait()
        logs = []
        for r in range(kv * group // per, (kv + 1) * group // per):
            terms = packed_ref[r, tokens : tokens + PAD, :].astype(jnp.float32)
            logs.append(LOG2E * (terms[0:1] + terms[1:2] + terms[2:3]))
        cols = slice(kv * DH, (kv + 1) * DH)
        k_near, v_near = near_ref[:tokens, cols], near_ref[tokens:, cols]
        sides = (
            (top, bias_top, jnp.concatenate([far_ref[:half, cols], k_near, k_own[top, cols]], axis=0),
             jnp.concatenate([far_ref[half:, cols], v_near, v_own[top, cols]], axis=0)),
            (low, bias_low, jnp.concatenate([k_near, k_own[:, cols]], axis=0),
             jnp.concatenate([v_near, v_own[:, cols]], axis=0)),
        )
        sums = []
        for side, (rows, bias, keys, vals) in enumerate(sides):
            val_sum = key_sum = 0.0
            for first in range(kv * group, (kv + 1) * group, RUN):
                heads = range(first, first + RUN)
                shifts = []
                for h in heads[::2]:
                    at = (h % per + side) * DH
                    shifts.append(logs[h // per - kv * group // per][:, at : at + DH])
                q_rows, g_rows = stacked_heads(q_ref, rows, heads), stacked_heads(g_ref, rows, heads)
                weights = weights_of(keys, q_rows, bias, shifts)
                val_sum += dot(weights.astype(jnp.bfloat16), g_rows, ((1,), (0,)))
                dscore = score_grads(weights, vals, g_rows, out_rows(packed_ref, rows, heads, per))
                key_sum += dot(dscore, q_rows, ((1,), (0,)))
                at = (side * width // DH + first) * half
                ds_ref[:, at : at + RUN * half] = dscore
            sums.append((key_sum * SCALE, val_sum))
        for i, own in enumerate((dk_own, dv_own)):
            one, two = sums[0][i], sums[1][i]
            far_out[i * half : (i + 1) * half, cols] = one[:half].astype(jnp.bfloat16)
            near_out[i * tokens : (i + 1) * tokens, cols] = (one[half : 3 * half] + two[:tokens]).astype(jnp.bfloat16)
            own[top, cols] = one[3 * half :] + two[tokens : tokens + half]
            own[low, cols] = two[tokens + half :]


def query_kernel(halo_ref, k_own, ds_ref, dq_ref):
    tokens, width = dq_ref.shape
    half = tokens // 2
    kv_heads = k_own.shape[1] // DH
    group = width // DH // kv_heads
    for kv in range(kv_heads):
        cols = slice(kv * DH, (kv + 1) * DH)
        sides = (
            jnp.concatenate([halo_ref[:, cols], k_own[:half, cols]], axis=0),
            jnp.concatenate([halo_ref[half:, cols], k_own[:, cols]], axis=0),
        )
        for side, keys in enumerate(sides):
            for first in range(kv * group, (kv + 1) * group, RUN):
                at = (side * width // DH + first) * half
                grad_q = (dot(ds_ref[:, at : at + RUN * half], keys, ((0,), (0,))) * SCALE).astype(jnp.bfloat16)
                for i in range(RUN):
                    out = slice((first + i) * DH, (first + i + 1) * DH)
                    dq_ref[side * half : (side + 1) * half, out] = grad_q[i * half : (i + 1) * half]


def call(kernel, name, outs, *args, flops, in_hbm=(), out_hbm=0, scratch=(), limit=24):
    smem = pl.BlockSpec(memory_space=pltpu.SMEM)
    vmem = pl.BlockSpec(memory_space=pltpu.VMEM)
    hbm = pl.BlockSpec(memory_space=pl.ANY)
    return pl.pallas_call(
        kernel,
        in_specs=[smem if a.ndim == 1 else vmem for a in args] + [hbm] * len(in_hbm),
        out_specs=[vmem] * (len(outs) - out_hbm) + [hbm] * out_hbm,
        out_shape=[jax.ShapeDtypeStruct(s, d) for s, d in outs],
        compiler_params=pltpu.CompilerParams(vmem_limit_bytes=limit * 1024 * 1024),
        cost_estimate=pl.CostEstimate(flops=flops, bytes_accessed=4 << 20, transcendentals=1 << 20),
        scratch_shapes=scratch,
        name=name,
    )(*args, *in_hbm)


def body(queries, keys, values, grad_out, attn_out, log_norm, doc_start):
    tokens, width = queries.shape
    kv_width = keys.shape[1]
    half = tokens // 2
    heads = width // DH
    ranks = lax.axis_size("ulysses")
    rank = lax.axis_index("ulysses")
    index = rank * lax.axis_size("blk") + lax.axis_index("blk")
    run_place = index % min(4, lax.axis_size("blk"))
    beyond = index - (ranks - 2) * lax.axis_size("blk")
    far_turns = (run_place == 1) | (beyond == 0)
    near_turns = ((run_place == 0) & (rank % 2 == 1)) | (beyond == 0)
    place = jnp.stack([index * tokens, far_turns, near_turns]).astype(jnp.int32)
    start = lax.dynamic_slice_in_dim(doc_start, rank, 1, 0)
    bf16, f32 = jnp.bfloat16, jnp.float32

    wide, both = (tokens, kv_width), (2 * tokens, kv_width)
    near, far = call(pair_kernel, "pair", [(both, bf16), (wide, bf16)], keys, values, flops=0)
    near, near_fixed = passed_on(near, 1)
    far, far_fixed = passed_on(far, 2)
    rank_width = attn_out.shape[2]
    step = ranks // 4
    block = lambda *shape: pl.BlockSpec((step,) + shape, lambda c: (c, 0, 0))
    packed = pl.pallas_call(
        pack_kernel,
        grid=(ranks // step,),
        in_specs=[block(tokens, rank_width), block(heads // ranks, tokens)],
        out_specs=block(tokens + PAD, rank_width),
        out_shape=jax.ShapeDtypeStruct((ranks, tokens + PAD, rank_width), bf16),
        name="pack",
    )(attn_out, log_norm)
    packed = lax.all_to_all(packed, "ulysses", split_axis=0, concat_axis=0, tiled=True)

    unit = 2 * heads * 8 * half * half * DH
    r_far, r_near, dk_own, dv_own, dscore, key_halo = call(
        key_value_kernel, "key_value_grads",
        [(wide, bf16), (both, bf16), (wide, f32), (wide, f32), ((4 * half, 2 * heads * half), bf16),
         ((3 * half, kv_width), bf16)],
        place, start, queries, grad_out, keys, values, in_hbm=(far, far_fixed, near, near_fixed, packed), flops=4 * unit,
        scratch=[pltpu.VMEM(wide, bf16), pltpu.VMEM(both, bf16), pltpu.VMEM(packed.shape, bf16),
                 pltpu.SemaphoreType.DMA((2 + kv_width // DH,))])
    r_far = shifted(r_far, -2)
    r_near = shifted(r_near, -1)
    (grad_queries,) = call(query_kernel, "query_grads", [(queries.shape, bf16)], key_halo, keys, dscore, flops=unit)

    def total(own, near_part, far_part):
        far_part = jnp.pad(far_part.astype(f32), ((half, 0), (0, 0)))
        return (own + near_part.astype(f32) + far_part).astype(bf16)

    return (grad_queries, total(dk_own, r_near[:tokens], r_far[:half]), total(dv_own, r_near[tokens:], r_far[half:]))


def solution(mesh):
    tokens_spec = P(AXES, None)
    return jax.shard_map(
        body,
        mesh=mesh,
        in_specs=(tokens_spec,) * 4 + (P(None, "blk", "ulysses"), P(None, "ulysses", "blk"), P(None, "blk")),
        out_specs=(tokens_spec,) * 3,
        check_vma=False,
    )
```

time: 103 us -> 84.6 us (0.82)
  the two profiles are of different devices: /device:TPU:30 before, /device:TPU:24 now
where the time goes in v2:
time: 84.6 us; the launch traced here: 84.3 us
  waiting for transfers between devices  46.2 us (55%)
  starting transfers between devices  24.5 us (29%)
  Pallas kernels  11.9 us (14%)
  other arithmetic  0.87 us (1%)
    ppermute x2, waiting for transfers between devices, passed_on(): return (arrived, lax.ppermute(arrived, AXES, across))  25.7 us
    ppermute x2, waiting for transfers between devices, shifted(): return lax.ppermute(value, AXES, pairs)  15.7 us
    all_to_all x1, starting transfers between devices, body(): lax.all_to_all(packed, 'ulysses', split_axis=0, concat_axis=0, tiled=True)  9.24 us
    pallas_call x3, Pallas kernels, call(): pl.pallas_call(kernel, in_specs=[smem if a.ndim == 1 else vmem for a in a...  8.38 us
    ppermute x2, starting transfers between devices, shifted(): return lax.ppermute(value, AXES, pairs)  7.99 us
    ppermute x2, waiting for transfers between devices, passed_on(): arrived = lax.ppermute(value, AXES, direct)  4.8 us
    ppermute x2, starting transfers between devices, passed_on(): arrived = lax.ppermute(value, AXES, direct)  4.7 us
    pallas_call x1, Pallas kernels, body(): pl.pallas_call(pack_kernel, grid=(ranks // step,), in_specs=[block(tokens...  3.55 us
  transfers between devices with their start and end apart: 7, of which 5 were waited for; matrix products, arithmetic and copies ran while one was open for 0% of the time, Pallas kernels for 3%

profile of v2, /device:TPU:24, one launch (start us, length us, event | category | flops | bytes accessed | tf_op | source)
XLA Modules:
  0.0 84.3 jit_solution(9107916031124310444)
XLA Ops:
  0.6 0.0 copy-start
  0.6 3.5 %pack.1 = bf16[8,144,512]{2,1,0:T(8,128)(2,1)} custom-call(bf16[8,128,512]{2,1,0:T(8,128)(2,1)} %o_ref.1, f32[8,4,128]{2,1,0:T(4,128)} %log_ref.1), custom_call_target="tpu_custom_call" | custom-call | tf_op jit(solution)/shard_map/pack/pallas_call | solution.py:250
  4.2 0.0 copy-start.3
  4.2 0.0 copy-start.4
  4.2 0.0 copy-start.2
  4.2 9.2 %all-to-all-start = ((bf16[8,144,512]{2,1,0:T(8,128)(2,1)}), bf16[8,144,512]{2,1,0:T(8,128)(2,1)S(1)}, u32[]{:S(2)}, u32[]{:S(2)}) async-start(bf16[8,144,512]{2,1,0:T(8,128)(2,1)} %pack.1), calls=%async_computation | async-start | bytes 2359296 | tf_op jit(solution)/shard_map/all_to_all | solution.py:258
  13.4 0.0 copy-done.3
  13.4 0.0 copy-done.4
  13.4 0.0 copy-start.1
  13.5 0.7 pair.1
  14.1 2.0 %collective-permute-start.2 = (bf16[256,512]{1,0:T(8,128)(2,1)S(1)}, bf16[256,512]{1,0:T(8,128)(2,1)}, u32[]{:S(2)}, u32[]{:S(2)}) collective-permute-start(bf16[256,512]{1,0:T(8,128)(2,1)S(1)} %get-tuple-element.12), channel_id=1, source_target_pairs={{0,1},{1,2},{2,3},{3,4},{4,5},{5,6},{6,7},{7,8},{8,9},{9,10},{10,1... | collective-permute-start | bytes 786440 | tf_op jit(solution)/shard_map/ppermute | solution.py:43
  16.1 2.7 %collective-permute-start = (bf16[128,512]{1,0:T(8,128)(2,1)}, bf16[128,512]{1,0:T(8,128)(2,1)}, u32[]{:S(2)}, u32[]{:S(2)}) collective-permute-start(bf16[128,512]{1,0:T(8,128)(2,1)} %get-tuple-element.11), channel_id=1, source_target_pairs={{0,2},{1,3},{2,4},{3,1},{4,6},{5,7},{6,8},{7,5},{8,10},{9,11},{10,... | collective-permute-start | bytes 393224 | tf_op jit(solution)/shard_map/ppermute | solution.py:43
  18.8 3.2 %collective-permute-done.2.near_hbm = bf16[256,512]{1,0:T(8,128)(2,1)} collective-permute-done((bf16[256,512]{1,0:T(8,128)(2,1)S(1)}, bf16[256,512]{1,0:T(8,128)(2,1)}, u32[]{:S(2)}, u32[]{:S(2)}) %collective-permute-start.2) | collective-permute-done | bytes 262176 | tf_op jit(solution)/shard_map/ppermute | solution.py:43
  22.0 1.3 %collective-permute-start.3 = (bf16[256,512]{1,0:T(8,128)(2,1)}, bf16[256,512]{1,0:T(8,128)(2,1)}, u32[]{:S(2)}, u32[]{:S(2)}) collective-permute-start(bf16[256,512]{1,0:T(8,128)(2,1)} %collective-permute-done.2.near_hbm), channel_id=1, source_target_pairs={{124,64},{64,68},{68,72},{72,76},{76,80},{80,84},{84,88},{88,92},{... | collective-permute-start | bytes 786440 | tf_op jit(solution)/shard_map/ppermute | solution.py:44
  23.3 1.6 %collective-permute-done.far_hbm = bf16[128,512]{1,0:T(8,128)(2,1)} collective-permute-done((bf16[128,512]{1,0:T(8,128)(2,1)}, bf16[128,512]{1,0:T(8,128)(2,1)}, u32[]{:S(2)}, u32[]{:S(2)}) %collective-permute-start) | collective-permute-done | bytes 131104 | tf_op jit(solution)/shard_map/ppermute | solution.py:43
  24.9 1.3 %collective-permute-start.1 = (bf16[128,512]{1,0:T(8,128)(2,1)}, bf16[128,512]{1,0:T(8,128)(2,1)}, u32[]{:S(2)}, u32[]{:S(2)}) collective-permute-start(bf16[128,512]{1,0:T(8,128)(2,1)} %collective-permute-done.far_hbm), channel_id=1, source_target_pairs={{1,5},{5,9},{9,13},{13,17},{17,21},{21,25},{25,29},{29,33},{33,37}... | collective-permute-start | bytes 393224 | tf_op jit(solution)/shard_map/ppermute | solution.py:44
  26.2 0.0 copy-done
  26.3 0.1 pad_add_fusion.place_ref
  26.4 25.7 %collective-permute-done.1.far_fixed = bf16[128,512]{1,0:T(8,128)(2,1)} collective-permute-done((bf16[128,512]{1,0:T(8,128)(2,1)}, bf16[128,512]{1,0:T(8,128)(2,1)}, u32[]{:S(2)}, u32[]{:S(2)}) %collective-permute-start.1) | collective-permute-done | bytes 131104 | tf_op jit(solution)/shard_map/ppermute | solution.py:44
  52.1 0.0 collective-permute-done.3.near_fixed
  52.1 0.0 all-to-all-done.packed_hbm
  52.1 0.0 copy-done.2
  52.1 0.0 copy-done.1
  52.1 5.9 %key_value_grads.1 = (bf16[128,512]{1,0:T(8,128)(2,1)S(1)}, bf16[256,512]{1,0:T(8,128)(2,1)S(1)}, f32[128,512]{1,0:T(8,128)S(1)}, f32[128,512]{1,0:T(8,128)S(1)}...) custom-call(s32[3]{0:T(128)S(1)} %pad_add_fusion.place_ref, ...), custom_call_target="tpu_custom_call" | custom-call | flops 1073741824 | bytes 4194304 | tf_op jit(solution)/shard_map/key_value_grads/pallas_call | solution.py:215
  58.0 3.3 %collective-permute-start.5 = (bf16[128,512]{1,0:T(8,128)(2,1)S(1)}, bf16[128,512]{1,0:T(8,128)(2,1)S(1)}, u32[]{:S(2)}, u32[]{:S(2)}) collective-permute-start(bf16[128,512]{1,0:T(8,128)(2,1)S(1)} %get-tuple-element.17), channel_id=1, source_target_pairs={{2,0},{3,1},{4,2},{5,3},{6,4},{7,5},{8,6},{9,7},{10,8},{11,9},{12,... | collective-permute-start | bytes 393224 | tf_op jit(solution)/shard_map/ppermute | solution.py:19
  61.3 4.7 %collective-permute-start.4 = (bf16[256,512]{1,0:T(8,128)(2,1)S(1)}, bf16[256,512]{1,0:T(8,128)(2,1)S(1)}, u32[]{:S(2)}, u32[]{:S(2)}) collective-permute-start(bf16[256,512]{1,0:T(8,128)(2,1)S(1)} %get-tuple-element.16), channel_id=1, source_target_pairs={{1,0},{2,1},{3,2},{4,3},{5,4},{6,5},{7,6},{8,7},{9,8},{10,9},{11,1... | collective-permute-start | bytes 786440 | tf_op jit(solution)/shard_map/ppermute | solution.py:19
  66.0 1.8 %query_grads.1 = bf16[128,4096]{1,0:T(8,128)(2,1)} custom-call(bf16[192,512]{1,0:T(8,128)(2,1)S(1)} %get-tuple-element.13.halo_ref, bf16[128,512]{1,0:T(8,128)(2,1)S(1)} %copy-done.3, bf16[256,4096]{1,0:T(8,128)(2,1)S(1)} %get-tuple-element.14.ds_ref), custom_call_target="tpu_custom_call" | custom-call | flops 268435456 | bytes 4194304 | tf_op jit(solution)/shard_map/query_grads/pallas_call | solution.py:215
  67.8 12.9 %collective-permute-done.5 = bf16[128,512]{1,0:T(8,128)(2,1)S(1)} collective-permute-done((bf16[128,512]{1,0:T(8,128)(2,1)S(1)}, bf16[128,512]{1,0:T(8,128)(2,1)S(1)}, u32[]{:S(2)}, u32[]{:S(2)}) %collective-permute-start.5) | collective-permute-done | bytes 131104 | tf_op jit(solution)/shard_map/ppermute | solution.py:19
  80.7 2.8 %collective-permute-done.4 = bf16[256,512]{1,0:T(8,128)(2,1)S(1)} collective-permute-done((bf16[256,512]{1,0:T(8,128)(2,1)S(1)}, bf16[256,512]{1,0:T(8,128)(2,1)S(1)}, u32[]{:S(2)}, u32[]{:S(2)}) %collective-permute-start.4) | collective-permute-done | bytes 262176 | tf_op jit(solution)/shard_map/ppermute | solution.py:19
  83.5 0.8 add_convert_fusion
  (2 shorter events, 0.0 us)
Async XLA Ops:
  0.6 25.6 %copy-start = (s32[8,128]{1,0:T(8,128)S(1)}, s32[8,128]{1,0:T(8,128)}, u32[]{:S(2)}) copy-start(s32[8,128]{1,0:T(8,128)} %param.13) | copy-start | bytes 12292
  4.2 9.2 %copy-start.3 = (bf16[128,512]{1,0:T(8,128)(2,1)S(1)}, bf16[128,512]{1,0:T(8,128)(2,1)}, u32[]{:S(2)}) copy-start(bf16[128,512]{1,0:T(8,128)(2,1)} %k_own.3) | copy-start | bytes 393220
  4.2 9.3 %copy-start.4 = (bf16[128,512]{1,0:T(8,128)(2,1)S(1)}, bf16[128,512]{1,0:T(8,128)(2,1)}, u32[]{:S(2)}) copy-start(bf16[128,512]{1,0:T(8,128)(2,1)} %v_own.1) | copy-start | bytes 393220
  4.2 47.9 %copy-start.2 = (bf16[128,4096]{1,0:T(8,128)(2,1)S(1)}, bf16[128,4096]{1,0:T(8,128)(2,1)}, u32[]{:S(2)}) copy-start(bf16[128,4096]{1,0:T(8,128)(2,1)} %g_ref.1) | copy-start | bytes 3145732
  4.2 47.9 %all-to-all-start = ((bf16[8,144,512]{2,1,0:T(8,128)(2,1)}), bf16[8,144,512]{2,1,0:T(8,128)(2,1)S(1)}, u32[]{:S(2)}, u32[]{:S(2)}) async-start(bf16[8,144,512]{2,1,0:T(8,128)(2,1)} %pack.1), calls=%async_computation | async-start | bytes 2359296 | tf_op jit(solution)/shard_map/all_to_all | solution.py:258
  13.4 38.6 %copy-start.1 = (bf16[128,4096]{1,0:T(8,128)(2,1)S(1)}, bf16[128,4096]{1,0:T(8,128)(2,1)}, u32[]{:S(2)}) copy-start(bf16[128,4096]{1,0:T(8,128)(2,1)} %q_ref.1) | copy-start | bytes 3145732
  14.1 7.9 %collective-permute-start.2 = (bf16[256,512]{1,0:T(8,128)(2,1)S(1)}, bf16[256,512]{1,0:T(8,128)(2,1)}, u32[]{:S(2)}, u32[]{:S(2)}) collective-permute-start(bf16[256,512]{1,0:T(8,128)(2,1)S(1)} %get-tuple-element.12), channel_id=1, source_target_pairs={{0,1},{1,2},{2,3},{3,4},{4,5},{5,6},{6,7},{7,8},{8,9},{9,10},{10,1... | collective-permute-start | bytes 786440 | tf_op jit(solution)/shard_map/ppermute | solution.py:43
  16.1 8.8 %collective-permute-start = (bf16[128,512]{1,0:T(8,128)(2,1)}, bf16[128,512]{1,0:T(8,128)(2,1)}, u32[]{:S(2)}, u32[]{:S(2)}) collective-permute-start(bf16[128,512]{1,0:T(8,128)(2,1)} %get-tuple-element.11), channel_id=1, source_target_pairs={{0,2},{1,3},{2,4},{3,1},{4,6},{5,7},{6,8},{7,5},{8,10},{9,11},{10,... | collective-permute-start | bytes 393224 | tf_op jit(solution)/shard_map/ppermute | solution.py:43
  22.0 30.1 %collective-permute-start.3 = (bf16[256,512]{1,0:T(8,128)(2,1)}, bf16[256,512]{1,0:T(8,128)(2,1)}, u32[]{:S(2)}, u32[]{:S(2)}) collective-permute-start(bf16[256,512]{1,0:T(8,128)(2,1)} %collective-permute-done.2.near_hbm), channel_id=1, source_target_pairs={{124,64},{64,68},{68,72},{72,76},{76,80},{80,84},{84,88},{88,92},{... | collective-permute-start | bytes 786440 | tf_op jit(solution)/shard_map/ppermute | solution.py:44
  24.9 27.1 %collective-permute-start.1 = (bf16[128,512]{1,0:T(8,128)(2,1)}, bf16[128,512]{1,0:T(8,128)(2,1)}, u32[]{:S(2)}, u32[]{:S(2)}) collective-permute-start(bf16[128,512]{1,0:T(8,128)(2,1)} %collective-permute-done.far_hbm), channel_id=1, source_target_pairs={{1,5},{5,9},{9,13},{13,17},{17,21},{21,25},{25,29},{29,33},{33,37}... | collective-permute-start | bytes 393224 | tf_op jit(solution)/shard_map/ppermute | solution.py:44
  58.0 22.7 %collective-permute-start.5 = (bf16[128,512]{1,0:T(8,128)(2,1)S(1)}, bf16[128,512]{1,0:T(8,128)(2,1)S(1)}, u32[]{:S(2)}, u32[]{:S(2)}) collective-permute-start(bf16[128,512]{1,0:T(8,128)(2,1)S(1)} %get-tuple-element.17), channel_id=1, source_target_pairs={{2,0},{3,1},{4,2},{5,3},{6,4},{7,5},{8,6},{9,7},{10,8},{11,9},{12,... | collective-permute-start | bytes 393224 | tf_op jit(solution)/shard_map/ppermute | solution.py:19
  61.3 22.1 %collective-permute-start.4 = (bf16[256,512]{1,0:T(8,128)(2,1)S(1)}, bf16[256,512]{1,0:T(8,128)(2,1)S(1)}, u32[]{:S(2)}, u32[]{:S(2)}) collective-permute-start(bf16[256,512]{1,0:T(8,128)(2,1)S(1)} %get-tuple-element.16), channel_id=1, source_target_pairs={{1,0},{2,1},{3,2},{4,3},{5,4},{6,5},{7,6},{8,7},{9,8},{10,9},{11,1... | collective-permute-start | bytes 786440 | tf_op jit(solution)/shard_map/ppermute | solution.py:19

commit v3 on v2

v3 whole, which is shorter than its diff:
```python
import jax
import jax.numpy as jnp
from jax import lax
from jax.experimental import pallas as pl
from jax.experimental.pallas import tpu as pltpu
from jax.sharding import PartitionSpec as P

DH = 128
AXES = ("ulysses", "blk")
LOG2E = 1.4426950408889634
SCALE = DH**-0.5
RUN = 4
PAD = 16


def shifted(value, steps):
    count = lax.axis_size("ulysses") * lax.axis_size("blk")
    pairs = [(s, s + steps) for s in range(count) if 0 <= s + steps < count]
    return lax.ppermute(value, AXES, pairs)


def routes(steps):
    ranks, blocks = lax.axis_size("ulysses"), lax.axis_size("blk")
    run = min(4, blocks)
    direct, across = [], []
    for source in range(ranks * blocks - steps):
        target = source + steps
        rank, place = divmod(source, blocks)
        if target == (ranks - 2) * blocks:
            direct.append((source, 0))
            across.append((0, target))
        elif place % run + steps == run + steps - 1 and (steps > 1 or target // blocks % 2 == 1):
            middle = (rank if steps > 1 else rank | 1) * blocks + place - run + steps
            direct.append((source, middle))
            across.append((middle, target))
        else:
            direct.append((source, target))
    return direct, across


def passed_on(value, steps):
    direct, across = routes(steps)
    arrived = lax.ppermute(value, AXES, direct)
    return arrived, lax.ppermute(arrived, AXES, across)


def dot(a, b, dims):
    return lax.dot_general(a, b, (dims, ((), ())), preferred_element_type=jnp.float32)


def pair_kernel(k_ref, v_ref, near_ref, far_ref):
    tokens = k_ref.shape[0]
    half = tokens // 2
    near_ref[:tokens] = k_ref[...]
    near_ref[tokens:] = v_ref[...]
    far_ref[:half] = k_ref[half:]
    far_ref[half:] = v_ref[half:]


def pack_kernel(log_ref, o_hbm, packed_hbm, packed, sems):
    count, per, tokens = log_ref.shape
    half = tokens // 2
    loads = [pltpu.make_async_copy(o_hbm.at[c], packed.at[c, pl.ds(0, tokens)], sems.at[0, c]) for c in range(count)]
    stores = [pltpu.make_async_copy(packed.at[c], packed_hbm.at[c], sems.at[1, c]) for c in range(count)]
    for load in loads:
        load.start()
    lane = lax.broadcasted_iota(jnp.int32, (1, tokens), 1)
    for c in range(count):
        rows = []
        for a in range(0, per, 2):
            one, two = log_ref[c, a : a + 1, :], log_ref[c, a + 1 : a + 2, :]
            rows.append(jnp.where(lane < half, one, pltpu.roll(two, half, 1)))
            rows.append(jnp.where(lane < half, pltpu.roll(one, half, 1), two))
        left = jnp.concatenate(rows, axis=1)
        terms = []
        for _ in range(3):
            term = left.astype(jnp.bfloat16).astype(jnp.float32)
            left = left - term
            terms.append(term)
        terms.append(jnp.zeros((PAD - 3, left.shape[1]), jnp.float32))
        packed[c, tokens:] = jnp.concatenate(terms, axis=0).astype(jnp.bfloat16)
        loads[c].wait()
        stores[c].start()
    for store in stores:
        store.wait()


def head_cols(ref, rows, head):
    return ref[rows, head * DH : (head + 1) * DH]


def stacked_heads(ref, rows, heads):
    return jnp.concatenate([head_cols(ref, rows, h) for h in heads], axis=0)


def out_rows(ref, rows, heads, per):
    return jnp.concatenate([ref[h // per, rows, h % per * DH : (h % per + 1) * DH] for h in heads], axis=0)


def mask_bias(place_ref, start_ref, first_key, first_query, span, half):
    tokens = 2 * half
    key = lax.broadcasted_iota(jnp.int32, (span, tokens), 0) + first_key
    lane = lax.broadcasted_iota(jnp.int32, (span, tokens), 1)
    query = lax.rem(lane, half) + first_query
    start = start_ref[...] - place_ref[0]
    low = lax.broadcasted_iota(jnp.int32, start.shape, 1) < half
    moved = pltpu.roll(start, half, 1)
    start = jnp.where(low, moved, start) if first_query else jnp.where(low, start, moved)
    allowed = (key <= query) & (key > query - 3 * tokens // 2) & (key >= start)
    return jnp.where(allowed, 0.0, -jnp.inf)


def weights_of(keys, q_rows, bias, rows):
    shift = jnp.concatenate([bias - row for row in rows], axis=1)
    return jnp.exp2(dot(keys, q_rows, ((1,), (1,))) * (SCALE * LOG2E) + shift)


def centre_cols(g_rows, o_rows):
    prod = g_rows.astype(jnp.float32) * o_rows.astype(jnp.float32)
    prod = prod + pltpu.roll(prod, DH // 2, 1)
    head = prod.astype(jnp.bfloat16).astype(jnp.float32)
    lane = lax.broadcasted_iota(jnp.int32, prod.shape, 1)
    return jnp.where(lane < DH // 2, head, prod - head).astype(jnp.bfloat16)


def score_grads(weights, vals, g_rows, o_rows):
    vals = jnp.concatenate([vals, jnp.full(vals.shape, -1.0, vals.dtype)], axis=1)
    both = jnp.concatenate([g_rows, centre_cols(g_rows, o_rows)], axis=1)
    return (weights * dot(vals, both, ((1,), (1,)))).astype(jnp.bfloat16)


def log_terms(packed_ref, ranks, tokens):
    logs = {}
    for r in ranks:
        terms = packed_ref[r, tokens : tokens + PAD, :].astype(jnp.float32)
        logs[r] = LOG2E * (terms[0:1] + terms[1:2] + terms[2:3])
    return logs


def run_grads(q_ref, g_ref, packed_ref, logs, side, heads, per, keys, vals, bias):
    half = q_ref.shape[0] // 2
    rows = slice(side * half, (side + 1) * half)
    shifts = []
    for h in heads[::2]:
        at = (h % per + side) * DH
        shifts.append(logs[h // per][:, at : at + DH])
    q_rows, g_rows = stacked_heads(q_ref, rows, heads), stacked_heads(g_ref, rows, heads)
    weights = weights_of(keys, q_rows, bias, shifts)
    dscore = score_grads(weights, vals, g_rows, out_rows(packed_ref, rows, heads, per))
    return weights.astype(jnp.bfloat16), dscore, q_rows, g_rows


def start_all(pairs, sems, first):
    copies = [pltpu.make_async_copy(a, b, sems.at[first + i]) for i, (a, b) in enumerate(pairs)]
    for copy in copies:
        copy.start()
    return copies


def packed_moves(packed_hbm, packed_ref, kv_heads):
    ranks = packed_ref.shape[0] // kv_heads
    return [(packed_hbm.at[pl.ds(kv * ranks, ranks)], packed_ref.at[pl.ds(kv * ranks, ranks)]) for kv in range(kv_heads)]


def halo_kernel(place_ref, start_ref, q_ref, g_ref, far_hbm, far_fixed, near_hbm, near_fixed, packed_hbm,
                far_out, near_out, keys_out, ds_top, ds_low, far_ref, near_ref, packed_ref, sems):
    tokens, width = q_ref.shape
    half = tokens // 2
    kv_heads = far_ref.shape[1] // DH
    group = width // DH // kv_heads
    per = width // DH // packed_ref.shape[0]
    sources = ((far_hbm, far_fixed, far_ref), (near_hbm, near_fixed, near_ref))
    for i, (direct, fixed, target) in enumerate(sources):
        staged = place_ref[1 + i] == 1
        pl.when(staged)(pltpu.make_async_copy(fixed, target, sems.at[i]).start)
        pl.when(jnp.logical_not(staged))(pltpu.make_async_copy(direct, target, sems.at[i]).start)
    copies = start_all(packed_moves(packed_hbm, packed_ref, kv_heads), sems, 2)
    biases = (mask_bias(place_ref, start_ref, -3 * half, 0, 3 * half, half),
              mask_bias(place_ref, start_ref, -2 * half, half, tokens, half))
    for i, (direct, _, target) in enumerate(sources):
        pltpu.make_async_copy(direct, target, sems.at[i]).wait()
    keys_out[:half] = far_ref[:half]
    keys_out[half:] = near_ref[:tokens]
    for kv in range(kv_heads):
        copies[kv].wait()
        logs = log_terms(packed_ref, range(kv * group // per, (kv + 1) * group // per), tokens)
        cols = slice(kv * DH, (kv + 1) * DH)
        k_near, v_near = near_ref[:tokens, cols], near_ref[tokens:, cols]
        keys = (jnp.concatenate([far_ref[:half, cols], k_near], axis=0), k_near)
        vals = (jnp.concatenate([far_ref[half:, cols], v_near], axis=0), v_near)
        sums = []
        for side, ds_ref in enumerate((ds_top, ds_low)):
            val_sum = key_sum = 0.0
            for first in range(kv * group, (kv + 1) * group, RUN):
                weights, dscore, q_rows, g_rows = run_grads(
                    q_ref, g_ref, packed_ref, logs, side, range(first, first + RUN), per, keys[side], vals[side], biases[side])
                val_sum += dot(weights, g_rows, ((1,), (0,)))
                key_sum += dot(dscore, q_rows, ((1,), (0,)))
                ds_ref[:, first * half : (first + RUN) * half] = dscore
            sums.append((key_sum * SCALE, val_sum))
        for i in range(2):
            one, two = sums[0][i], sums[1][i]
            far_out[i * half : (i + 1) * half, cols] = one[:half].astype(jnp.bfloat16)
            near_out[i * tokens : (i + 1) * tokens, cols] = (one[half:] + two).astype(jnp.bfloat16)


def own_kernel(place_ref, start_ref, q_ref, g_ref, k_own, v_own, halo_ref, ds_top, ds_low, packed_hbm,
               dk_own, dv_own, dq_ref, packed_ref, sems):
    tokens, width = q_ref.shape
    half = tokens // 2
    kv_heads = k_own.shape[1] // DH
    group = width // DH // kv_heads
    per = width // DH // packed_ref.shape[0]
    copies = start_all(packed_moves(packed_hbm, packed_ref, kv_heads), sems, 0)
    biases = (mask_bias(place_ref, start_ref, 0, 0, half, half), mask_bias(place_ref, start_ref, 0, half, tokens, half))
    for kv in range(kv_heads):
        copies[kv].wait()
        logs = log_terms(packed_ref, range(kv * group // per, (kv + 1) * group // per), tokens)
        cols = slice(kv * DH, (kv + 1) * DH)
        sums = []
        for side, ds_ref in enumerate((ds_top, ds_low)):
            keys, vals = k_own[: (side + 1) * half, cols], v_own[: (side + 1) * half, cols]
            all_keys = jnp.concatenate([halo_ref[side * half :, cols], keys], axis=0)
            val_sum = key_sum = 0.0
            for first in range(kv * group, (kv + 1) * group, RUN):
                weights, dscore, q_rows, g_rows = run_grads(
                    q_ref, g_ref, packed_ref, logs, side, range(first, first + RUN), per, keys, vals, biases[side])
                val_sum += dot(weights, g_rows, ((1,), (0,)))
                key_sum += dot(dscore, q_rows, ((1,), (0,)))
                dscore = jnp.concatenate([ds_ref[:, first * half : (first + RUN) * half], dscore], axis=0)
                grad_q = (dot(dscore, all_keys, ((0,), (0,))) * SCALE).astype(jnp.bfloat16)
                for i in range(RUN):
                    out = slice((first + i) * DH, (first + i + 1) * DH)
                    dq_ref[side * half : (side + 1) * half, out] = grad_q[i * half : (i + 1) * half]
            sums.append((key_sum * SCALE, val_sum))
        for i, own in enumerate((dk_own, dv_own)):
            one, two = sums[0][i], sums[1][i]
            own[:half, cols] = one + two[:half]
            own[half:, cols] = two[half:]


def call(kernel, name, outs, *args, flops, in_hbm=(), out_hbm=0, scratch=(), limit=24):
    smem = pl.BlockSpec(memory_space=pltpu.SMEM)
    vmem = pl.BlockSpec(memory_space=pltpu.VMEM)
    hbm = pl.BlockSpec(memory_space=pl.ANY)
    return pl.pallas_call(
        kernel,
        in_specs=[smem if a.ndim == 1 else vmem for a in args] + [hbm] * len(in_hbm),
        out_specs=[vmem] * (len(outs) - out_hbm) + [hbm] * out_hbm,
        out_shape=[jax.ShapeDtypeStruct(s, d) for s, d in outs],
        compiler_params=pltpu.CompilerParams(vmem_limit_bytes=limit * 1024 * 1024),
        cost_estimate=pl.CostEstimate(flops=flops, bytes_accessed=4 << 20, transcendentals=1 << 20),
        scratch_shapes=scratch,
        name=name,
    )(*args, *in_hbm)


def body(queries, keys, values, grad_out, attn_out, log_norm, doc_start):
    tokens, width = queries.shape
    kv_width = keys.shape[1]
    half = tokens // 2
    heads = width // DH
    ranks = lax.axis_size("ulysses")
    rank = lax.axis_index("ulysses")
    index = rank * lax.axis_size("blk") + lax.axis_index("blk")
    run_place = index % min(4, lax.axis_size("blk"))
    beyond = index - (ranks - 2) * lax.axis_size("blk")
    far_turns = (run_place == 1) | (beyond == 0)
    near_turns = ((run_place == 0) & (rank % 2 == 1)) | (beyond == 0)
    place = jnp.stack([index * tokens, far_turns, near_turns]).astype(jnp.int32)
    start = lax.dynamic_slice_in_dim(doc_start, rank, 1, 0)
    bf16, f32 = jnp.bfloat16, jnp.float32

    wide, both = (tokens, kv_width), (2 * tokens, kv_width)
    near, far = call(pair_kernel, "pair", [(both, bf16), (wide, bf16)], keys, values, flops=0)
    near, near_fixed = passed_on(near, 1)
    far, far_fixed = passed_on(far, 2)
    sent = (ranks, tokens + PAD, attn_out.shape[2])
    (packed,) = call(
        pack_kernel, "pack", [(sent, bf16)], log_norm, in_hbm=(attn_out,), out_hbm=1, flops=0, limit=60,
        scratch=[pltpu.VMEM(sent, bf16), pltpu.SemaphoreType.DMA((2, ranks))])
    packed = lax.all_to_all(packed, "ulysses", split_axis=0, concat_axis=0, tiled=True)

    unit = 2 * heads * 8 * half * half * DH
    packed_scratch = [pltpu.VMEM(packed.shape, bf16), pltpu.SemaphoreType.DMA((2 + kv_width // DH,))]
    r_far, r_near, key_halo, ds_top, ds_low = call(
        halo_kernel, "halo_grads",
        [(wide, bf16), (both, bf16), ((3 * half, kv_width), bf16), ((3 * half, heads * half), bf16),
         ((tokens, heads * half), bf16)],
        place, start, queries, grad_out, in_hbm=(far, far_fixed, near, near_fixed, packed), flops=3 * unit,
        scratch=[pltpu.VMEM(wide, bf16), pltpu.VMEM(both, bf16)] + packed_scratch)
    r_far = shifted(r_far, -2)
    r_near = shifted(r_near, -1)
    dk_own, dv_own, grad_queries = call(
        own_kernel, "own_grads", [(wide, f32), (wide, f32), (queries.shape, bf16)],
        place, start, queries, grad_out, keys, values, key_halo, ds_top, ds_low, in_hbm=(packed,), flops=3 * unit,
        scratch=packed_scratch)
    r_far = r_far.astype(f32)

    def total(own, near_part, far_part):
        return (own + near_part.astype(f32) + jnp.pad(far_part, ((half, 0), (0, 0)))).astype(bf16)

    return (grad_queries, total(dk_own, r_near[:tokens], r_far[:half]), total(dv_own, r_near[tokens:], r_far[half:]))


def solution(mesh):
    tokens_spec = P(AXES, None)
    return jax.shard_map(
        body,
        mesh=mesh,
        in_specs=(tokens_spec,) * 4 + (P(None, "blk", "ulysses"), P(None, "ulysses", "blk"), P(None, "blk")),
        out_specs=(tokens_spec,) * 3,
        check_vma=False,
    )
```

time: 84.6 us -> 82.8 us (0.979)
  waiting for transfers between devices: 46.2 us -> 40.3 us
  Pallas kernels: 11.9 us -> 15.7 us
    pallas_call x3 -> x4, Pallas kernels: 8.38 us -> 15.7 us  [call(): pl.pallas_call(kernel, in_specs=[smem if a.ndim == 1 else vmem for a in a...]
    ppermute x2, waiting for transfers between devices: 15.7 us -> 10.1 us  [shifted(): return lax.ppermute(value, AXES, pairs)]
    pallas_call x1 -> x0, Pallas kernels: 3.55 us -> none  [body(): pl.pallas_call(pack_kernel, grid=(ranks // step,), in_specs=[block(tokens...]
  transfers between devices with their start and end apart: 7 -> 7, of which waited for: 5 -> 5; matrix products, arithmetic and copies ran while one was open for 0% -> 0% of each run, Pallas kernels for 3% -> 10%
where the time goes in v3:
time: 82.8 us; the launch traced here: 82.4 us
  waiting for transfers between devices  40.3 us (49%)
  starting transfers between devices  24.7 us (30%)
  Pallas kernels  15.7 us (19%)
  other arithmetic  0.88 us (1%)
  between operations  0.85 us (1%)
    ppermute x2, waiting for transfers between devices, passed_on(): return (arrived, lax.ppermute(arrived, AXES, across))  25.4 us
    pallas_call x4, Pallas kernels, call(): pl.pallas_call(kernel, in_specs=[smem if a.ndim == 1 else vmem for a in a...  15.7 us
    ppermute x2, waiting for transfers between devices, shifted(): return lax.ppermute(value, AXES, pairs)  10.1 us
    all_to_all x1, starting transfers between devices, body(): lax.all_to_all(packed, 'ulysses', split_axis=0, concat_axis=0, tiled=True)  9.24 us
    ppermute x2, starting transfers between devices, shifted(): return lax.ppermute(value, AXES, pairs)  8.19 us
    ppermute x2, waiting for transfers between devices, passed_on(): arrived = lax.ppermute(value, AXES, direct)  4.8 us
    ppermute x2, starting transfers between devices, passed_on(): arrived = lax.ppermute(value, AXES, direct)  4.69 us
    ppermute x2, starting transfers between devices, passed_on(): return (arrived, lax.ppermute(arrived, AXES, across))  2.56 us
  transfers between devices with their start and end apart: 7, of which 5 were waited for; matrix products, arithmetic and copies ran while one was open for 0% of the time, Pallas kernels for 10%

profile of v3, /device:TPU:24, one launch (start us, length us, event | category | flops | bytes accessed | tf_op | source)
XLA Modules:
  0.0 82.4 jit_solution(1729154962812779699)
XLA Ops:
  0.6 0.0 copy-start
  0.6 3.0 %pack.1 = bf16[8,144,512]{2,1,0:T(8,128)(2,1)} custom-call(f32[8,4,128]{2,1,0:T(4,128)} %log_ref.1, bf16[8,128,512]{2,1,0:T(8,128)(2,1)} %o_hbm.1), custom_call_target="tpu_custom_call" | custom-call | bytes 4194304 | tf_op jit(solution)/shard_map/pack/pallas_call | solution.py:246
  3.7 0.0 copy-start.3
  3.7 0.0 copy-start.5
  3.7 0.0 copy-start.2
  3.7 9.2 %all-to-all-start = ((bf16[8,144,512]{2,1,0:T(8,128)(2,1)}), bf16[8,144,512]{2,1,0:T(8,128)(2,1)S(1)}, u32[]{:S(2)}, u32[]{:S(2)}) async-start(bf16[8,144,512]{2,1,0:T(8,128)(2,1)} %pack.1), calls=%async_computation | async-start | bytes 2359296 | tf_op jit(solution)/shard_map/all_to_all | solution.py:282
  12.9 0.0 copy-done.3
  12.9 0.0 copy-done.5
  12.9 0.0 copy-start.1
  13.0 0.7 pair.1
  13.6 1.3 %collective-permute-start.2 = (bf16[256,512]{1,0:T(8,128)(2,1)S(1)}, bf16[256,512]{1,0:T(8,128)(2,1)S(1)}, u32[]{:S(2)}, u32[]{:S(2)}) collective-permute-start(bf16[256,512]{1,0:T(8,128)(2,1)S(1)} %get-tuple-element.14), channel_id=1, source_target_pairs={{0,1},{1,2},{2,3},{3,4},{4,5},{5,6},{6,7},{7,8},{8,9},{9,10},{10,1... | collective-permute-start | bytes 786440 | tf_op jit(solution)/shard_map/ppermute | solution.py:43
  14.9 3.4 %collective-permute-start = (bf16[128,512]{1,0:T(8,128)(2,1)}, bf16[128,512]{1,0:T(8,128)(2,1)}, u32[]{:S(2)}, u32[]{:S(2)}) collective-permute-start(bf16[128,512]{1,0:T(8,128)(2,1)} %get-tuple-element.13), channel_id=1, source_target_pairs={{0,2},{1,3},{2,4},{3,1},{4,6},{5,7},{6,8},{7,5},{8,10},{9,11},{10,... | collective-permute-start | bytes 393224 | tf_op jit(solution)/shard_map/ppermute | solution.py:43
  18.3 3.2 %collective-permute-done.2.near_hbm = bf16[256,512]{1,0:T(8,128)(2,1)S(1)} collective-permute-done((bf16[256,512]{1,0:T(8,128)(2,1)S(1)}, bf16[256,512]{1,0:T(8,128)(2,1)S(1)}, u32[]{:S(2)}, u32[]{:S(2)}) %collective-permute-start.2) | collective-permute-done | bytes 262176 | tf_op jit(solution)/shard_map/ppermute | solution.py:43
  21.5 1.3 %collective-permute-start.3 = (bf16[256,512]{1,0:T(8,128)(2,1)S(1)}, bf16[256,512]{1,0:T(8,128)(2,1)}, u32[]{:S(2)}, u32[]{:S(2)}) collective-permute-start(bf16[256,512]{1,0:T(8,128)(2,1)S(1)} %collective-permute-done.2.near_hbm), channel_id=1, source_target_pairs={{124,64},{64,68},{68,72},{72,76},{76,80},{80,84},{84,88},{88,92},{... | collective-permute-start | bytes 786440 | tf_op jit(solution)/shard_map/ppermute | solution.py:44
  22.8 1.6 %collective-permute-done.far_hbm = bf16[128,512]{1,0:T(8,128)(2,1)} collective-permute-done((bf16[128,512]{1,0:T(8,128)(2,1)}, bf16[128,512]{1,0:T(8,128)(2,1)}, u32[]{:S(2)}, u32[]{:S(2)}) %collective-permute-start) | collective-permute-done | bytes 131104 | tf_op jit(solution)/shard_map/ppermute | solution.py:43
  24.4 1.3 %collective-permute-start.1 = (bf16[128,512]{1,0:T(8,128)(2,1)}, bf16[128,512]{1,0:T(8,128)(2,1)}, u32[]{:S(2)}, u32[]{:S(2)}) collective-permute-start(bf16[128,512]{1,0:T(8,128)(2,1)} %collective-permute-done.far_hbm), channel_id=1, source_target_pairs={{1,5},{5,9},{9,13},{13,17},{17,21},{21,25},{25,29},{29,33},{33,37}... | collective-permute-start | bytes 393224 | tf_op jit(solution)/shard_map/ppermute | solution.py:44
  25.7 0.0 copy-done
  25.8 0.1 pad_add_fusion.place_ref
  25.9 25.4 %collective-permute-done.1.far_fixed = bf16[128,512]{1,0:T(8,128)(2,1)} collective-permute-done((bf16[128,512]{1,0:T(8,128)(2,1)}, bf16[128,512]{1,0:T(8,128)(2,1)}, u32[]{:S(2)}, u32[]{:S(2)}) %collective-permute-start.1) | collective-permute-done | bytes 131104 | tf_op jit(solution)/shard_map/ppermute | solution.py:44
  51.3 0.0 collective-permute-done.3.near_fixed
  51.3 0.0 all-to-all-done.packed_hbm
  51.3 0.0 copy-done.2
  51.3 0.0 copy-done.1
  51.3 0.0 copy-start.4
  51.3 0.0 copy-start.6
  51.3 4.7 %halo_grads.1 = (bf16[128,512]{1,0:T(8,128)(2,1)S(1)}, bf16[256,512]{1,0:T(8,128)(2,1)S(1)}, bf16[192,512]{1,0:T(8,128)(2,1)S(1)}, bf16[192,2048]{1,0:T(8,128)(2,1)S(1)}, bf16[128,2048]{1,0:T(8,128)(2,1)S(1)}) custom-call(s32[3]{0:T(128)S(1)} %pad_add_fusion.place_ref, s32[1,128]{1,0:T(1,128)S(1)} %constant_dynamic-slice_fusion.start_ref, ...), custom_call_target="tpu_custom_call" | custom-call | flops 805306368 | bytes 4194304 | tf_op jit(solution)/shard_map/halo_grads/pallas_call | solution.py:246
  56.0 3.5 %collective-permute-start.5 = (bf16[128,512]{1,0:T(8,128)(2,1)S(1)}, bf16[128,512]{1,0:T(8,128)(2,1)S(1)}, u32[]{:S(2)}, u32[]{:S(2)}) collective-permute-start(bf16[128,512]{1,0:T(8,128)(2,1)S(1)} %get-tuple-element.21), channel_id=1, source_target_pairs={{2,0},{3,1},{4,2},{5,3},{6,4},{7,5},{8,6},{9,7},{10,8},{11,9},{12,... | collective-permute-start | bytes 393224 | tf_op jit(solution)/shard_map/ppermute | solution.py:19
  59.5 4.7 %collective-permute-start.4 = (bf16[256,512]{1,0:T(8,128)(2,1)S(1)}, bf16[256,512]{1,0:T(8,128)(2,1)S(1)}, u32[]{:S(2)}, u32[]{:S(2)}) collective-permute-start(bf16[256,512]{1,0:T(8,128)(2,1)S(1)} %get-tuple-element.20), channel_id=1, source_target_pairs={{1,0},{2,1},{3,2},{4,3},{5,4},{6,5},{7,6},{8,7},{9,8},{10,9},{11,1... | collective-permute-start | bytes 786440 | tf_op jit(solution)/shard_map/ppermute | solution.py:19
  64.2 0.0 copy-done.4
  64.2 0.0 copy-done.6
  64.2 7.3 %own_grads.1 = (f32[128,512]{1,0:T(8,128)S(1)}, f32[128,512]{1,0:T(8,128)S(1)}, bf16[128,4096]{1,0:T(8,128)(2,1)}) custom-call(s32[3]{0:T(128)S(1)} %pad_add_fusion.place_ref, s32[1,128]{1,0:T(1,128)S(1)} %constant_dynamic-slice_fusion.start_ref, bf16[128,4096]{1,0:T(8,128)(2,1)S(1)} %copy-done.1, bf16[128,4096]{1,0:T(8,128)(2,1)S(1)} %copy-done.2, ...), custom_call_target="tpu_custom_call" | custom-call | flops 805306368 | bytes 4194304 | tf_op jit(solution)/shard_map/own_grads/pallas_call | solution.py:246
  71.5 7.3 %collective-permute-done.5 = bf16[128,512]{1,0:T(8,128)(2,1)S(1)} collective-permute-done((bf16[128,512]{1,0:T(8,128)(2,1)S(1)}, bf16[128,512]{1,0:T(8,128)(2,1)S(1)}, u32[]{:S(2)}, u32[]{:S(2)}) %collective-permute-start.5) | collective-permute-done | bytes 131104 | tf_op jit(solution)/shard_map/ppermute | solution.py:19
  78.9 2.8 %collective-permute-done.4 = bf16[256,512]{1,0:T(8,128)(2,1)S(1)} collective-permute-done((bf16[256,512]{1,0:T(8,128)(2,1)S(1)}, bf16[256,512]{1,0:T(8,128)(2,1)S(1)}, u32[]{:S(2)}, u32[]{:S(2)}) %collective-permute-start.4) | collective-permute-done | bytes 262176 | tf_op jit(solution)/shard_map/ppermute | solution.py:19
  81.6 0.8 add_convert_fusion
  (2 shorter events, 0.0 us)
Async XLA Ops:
  0.6 25.1 %copy-start = (s32[8,128]{1,0:T(8,128)S(1)}, s32[8,128]{1,0:T(8,128)}, u32[]{:S(2)}) copy-start(s32[8,128]{1,0:T(8,128)} %param.13) | copy-start | bytes 12292
  3.7 9.3 %copy-start.3 = (bf16[128,512]{1,0:T(8,128)(2,1)S(1)}, bf16[128,512]{1,0:T(8,128)(2,1)}, u32[]{:S(2)}) copy-start(bf16[128,512]{1,0:T(8,128)(2,1)} %k_own.1) | copy-start | bytes 393220
  3.7 9.3 %copy-start.5 = (bf16[128,512]{1,0:T(8,128)(2,1)S(1)}, bf16[128,512]{1,0:T(8,128)(2,1)}, u32[]{:S(2)}) copy-start(bf16[128,512]{1,0:T(8,128)(2,1)} %v_own.1) | copy-start | bytes 393220
  3.7 47.6 %copy-start.2 = (bf16[128,4096]{1,0:T(8,128)(2,1)S(1)}, bf16[128,4096]{1,0:T(8,128)(2,1)}, u32[]{:S(2)}) copy-start(bf16[128,4096]{1,0:T(8,128)(2,1)} %g_ref.3) | copy-start | bytes 3145732
  3.7 47.6 %all-to-all-start = ((bf16[8,144,512]{2,1,0:T(8,128)(2,1)}), bf16[8,144,512]{2,1,0:T(8,128)(2,1)S(1)}, u32[]{:S(2)}, u32[]{:S(2)}) async-start(bf16[8,144,512]{2,1,0:T(8,128)(2,1)} %pack.1), calls=%async_computation | async-start | bytes 2359296 | tf_op jit(solution)/shard_map/all_to_all | solution.py:282
  12.9 38.3 %copy-start.1 = (bf16[128,4096]{1,0:T(8,128)(2,1)S(1)}, bf16[128,4096]{1,0:T(8,128)(2,1)}, u32[]{:S(2)}) copy-start(bf16[128,4096]{1,0:T(8,128)(2,1)} %q_ref.3) | copy-start | bytes 3145732
  13.6 7.9 %collective-permute-start.2 = (bf16[256,512]{1,0:T(8,128)(2,1)S(1)}, bf16[256,512]{1,0:T(8,128)(2,1)S(1)}, u32[]{:S(2)}, u32[]{:S(2)}) collective-permute-start(bf16[256,512]{1,0:T(8,128)(2,1)S(1)} %get-tuple-element.14), channel_id=1, source_target_pairs={{0,1},{1,2},{2,3},{3,4},{4,5},{5,6},{6,7},{7,8},{8,9},{9,10},{10,1... | collective-permute-start | bytes 786440 | tf_op jit(solution)/shard_map/ppermute | solution.py:43
  14.9 9.5 %collective-permute-start = (bf16[128,512]{1,0:T(8,128)(2,1)}, bf16[128,512]{1,0:T(8,128)(2,1)}, u32[]{:S(2)}, u32[]{:S(2)}) collective-permute-start(bf16[128,512]{1,0:T(8,128)(2,1)} %get-tuple-element.13), channel_id=1, source_target_pairs={{0,2},{1,3},{2,4},{3,1},{4,6},{5,7},{6,8},{7,5},{8,10},{9,11},{10,... | collective-permute-start | bytes 393224 | tf_op jit(solution)/shard_map/ppermute | solution.py:43
  21.5 29.7 %collective-permute-start.3 = (bf16[256,512]{1,0:T(8,128)(2,1)S(1)}, bf16[256,512]{1,0:T(8,128)(2,1)}, u32[]{:S(2)}, u32[]{:S(2)}) collective-permute-start(bf16[256,512]{1,0:T(8,128)(2,1)S(1)} %collective-permute-done.2.near_hbm), channel_id=1, source_target_pairs={{124,64},{64,68},{68,72},{72,76},{76,80},{80,84},{84,88},{88,92},{... | collective-permute-start | bytes 786440 | tf_op jit(solution)/shard_map/ppermute | solution.py:44
  24.4 26.8 %collective-permute-start.1 = (bf16[128,512]{1,0:T(8,128)(2,1)}, bf16[128,512]{1,0:T(8,128)(2,1)}, u32[]{:S(2)}, u32[]{:S(2)}) collective-permute-start(bf16[128,512]{1,0:T(8,128)(2,1)} %collective-permute-done.far_hbm), channel_id=1, source_target_pairs={{1,5},{5,9},{9,13},{13,17},{17,21},{21,25},{25,29},{29,33},{33,37}... | collective-permute-start | bytes 393224 | tf_op jit(solution)/shard_map/ppermute | solution.py:44
  51.3 12.9 %copy-start.4 = (bf16[128,512]{1,0:T(8,128)(2,1)S(1)}, bf16[128,512]{1,0:T(8,128)(2,1)}, u32[]{:S(2)}) copy-start(bf16[128,512]{1,0:T(8,128)(2,1)} %k_own.1) | copy-start | bytes 393220
  51.3 12.9 %copy-start.6 = (bf16[128,512]{1,0:T(8,128)(2,1)S(1)}, bf16[128,512]{1,0:T(8,128)(2,1)}, u32[]{:S(2)}) copy-start(bf16[128,512]{1,0:T(8,128)(2,1)} %v_own.1) | copy-start | bytes 393220
  56.0 22.9 %collective-permute-start.5 = (bf16[128,512]{1,0:T(8,128)(2,1)S(1)}, bf16[128,512]{1,0:T(8,128)(2,1)S(1)}, u32[]{:S(2)}, u32[]{:S(2)}) collective-permute-start(bf16[128,512]{1,0:T(8,128)(2,1)S(1)} %get-tuple-element.21), channel_id=1, source_target_pairs={{2,0},{3,1},{4,2},{5,3},{6,4},{7,5},{8,6},{9,7},{10,8},{11,9},{12,... | collective-permute-start | bytes 393224 | tf_op jit(solution)/shard_map/ppermute | solution.py:19
  59.5 22.1 %collective-permute-start.4 = (bf16[256,512]{1,0:T(8,128)(2,1)S(1)}, bf16[256,512]{1,0:T(8,128)(2,1)S(1)}, u32[]{:S(2)}, u32[]{:S(2)}) collective-permute-start(bf16[256,512]{1,0:T(8,128)(2,1)S(1)} %get-tuple-element.20), channel_id=1, source_target_pairs={{1,0},{2,1},{3,2},{4,3},{5,4},{6,5},{7,6},{8,7},{9,8},{10,9},{11,1... | collective-permute-start | bytes 786440 | tf_op jit(solution)/shard_map/ppermute | solution.py:19

commit v4 on v3

--- a/solution.py
+++ b/solution.py
@@ -290,11 +290,16 @@
         place, start, queries, grad_out, in_hbm=(far, far_fixed, near, near_fixed, packed), flops=3 * unit,
         scratch=[pltpu.VMEM(wide, bf16), pltpu.VMEM(both, bf16)] + packed_scratch)
     r_far = shifted(r_far, -2)
-    r_near = shifted(r_near, -1)
+    count, slow = ranks * lax.axis_size("blk"), (ranks - 2) * lax.axis_size("blk")
+    back = [(b, b - 1 if b != slow else count - 1) for b in range(1, count)]
+    r_near = lax.ppermute(r_near, AXES, back)
     dk_own, dv_own, grad_queries = call(
         own_kernel, "own_grads", [(wide, f32), (wide, f32), (queries.shape, bf16)],
         place, start, queries, grad_out, keys, values, key_halo, ds_top, ds_low, in_hbm=(packed,), flops=3 * unit,
         scratch=packed_scratch)
+    r_near, r_far, dk_own = lax.optimization_barrier((r_near, r_far, dk_own))
+    relayed = lax.ppermute(r_near, AXES, [(count - 1, slow - 1)])
+    r_near = jnp.where(index == slow - 1, relayed, jnp.where(index == count - 1, jnp.zeros_like(r_near), r_near))
     r_far = r_far.astype(f32)
 
     def total(own, near_part, far_part):

time: 82.8 us -> 81.9 us (0.989)
  waiting for transfers between devices: 40.3 us -> 36 us
  local copies, waits for them, and re-layouts: 0.08 us -> 2.29 us
  other arithmetic: 0.88 us -> 1.87 us
    ppermute x0 -> x2, starting transfers between devices: none -> 4.53 us  [the longest x1 3.86 us: body(): r_near = lax.ppermute(r_near, AXES, back)]
    ppermute x2 -> x1, starting transfers between devices: 8.19 us -> 3.73 us  [shifted(): return lax.ppermute(value, AXES, pairs)]
    ppermute x2 -> x1, waiting for transfers between devices: 10.1 us -> 5.77 us  [shifted(): return lax.ppermute(value, AXES, pairs)]
    unnamed x14 -> x20, local copies, waits for them, and re-layouts: 0.05 us -> 1.39 us
    select_n x0 -> x1, other arithmetic: none -> 0.99 us  [body(): jnp.where(index == slow - 1, relayed, jnp.where(index == count - 1, jnp.z...]
    slice x1, local copies, waits for them, and re-layouts: 0.02 us -> 0.89 us  [body(): r_far[half:]]
  transfers between devices with their start and end apart: 7 -> 8, of which waited for: 5 -> 4; matrix products, arithmetic and copies ran while one was open for 0% -> 1% of each run, Pallas kernels for 10% -> 10%
where the time goes in v4:
time: 81.9 us; the launch traced here: 81.4 us
  waiting for transfers between devices  36 us (44%)
  starting transfers between devices  24.7 us (30%)
  Pallas kernels  15.7 us (19%)
  local copies, waits for them, and re-layouts  2.29 us (3%)
  other arithmetic  1.87 us (2%)
  between operations  0.89 us (1%)
    ppermute x2, waiting for transfers between devices, passed_on(): return (arrived, lax.ppermute(arrived, AXES, across))  25.4 us
    pallas_call x4, Pallas kernels, call(): pl.pallas_call(kernel, in_specs=[smem if a.ndim == 1 else vmem for a in a...  15.7 us
    all_to_all x1, starting transfers between devices, body(): lax.all_to_all(packed, 'ulysses', split_axis=0, concat_axis=0, tiled=True)  9.24 us
    ppermute x1, waiting for transfers between devices, shifted(): return lax.ppermute(value, AXES, pairs)  5.77 us
    ppermute x2, waiting for transfers between devices, passed_on(): arrived = lax.ppermute(value, AXES, direct)  4.82 us
    ppermute x2, starting transfers between devices, passed_on(): arrived = lax.ppermute(value, AXES, direct)  4.67 us
    ppermute x1, starting transfers between devices, body(): r_near = lax.ppermute(r_near, AXES, back)  3.86 us
    ppermute x1, starting transfers between devices, shifted(): return lax.ppermute(value, AXES, pairs)  3.73 us
  transfers between devices with their start and end apart: 8, of which 4 were waited for; matrix products, arithmetic and copies ran while one was open for 1% of the time, Pallas kernels for 10%

profile of v4, /device:TPU:24, one launch (start us, length us, event | category | flops | bytes accessed | tf_op | source)
XLA Modules:
  0.0 81.4 jit_solution(190970372155243741)
XLA Ops:
  0.6 0.0 copy-start
  0.6 3.0 %pack.1 = bf16[8,144,512]{2,1,0:T(8,128)(2,1)} custom-call(f32[8,4,128]{2,1,0:T(4,128)} %log_ref.1, bf16[8,128,512]{2,1,0:T(8,128)(2,1)} %o_hbm.1), custom_call_target="tpu_custom_call" | custom-call | bytes 4194304 | tf_op jit(solution)/shard_map/pack/pallas_call | solution.py:246
  3.7 0.0 copy-start.5
  3.7 0.0 copy-start.7
  3.7 0.0 copy-start.2
  3.7 9.2 %all-to-all-start = ((bf16[8,144,512]{2,1,0:T(8,128)(2,1)}), bf16[8,144,512]{2,1,0:T(8,128)(2,1)S(1)}, u32[]{:S(2)}, u32[]{:S(2)}) async-start(bf16[8,144,512]{2,1,0:T(8,128)(2,1)} %pack.1), calls=%async_computation | async-start | bytes 2359296 | tf_op jit(solution)/shard_map/all_to_all | solution.py:282
  12.9 0.0 copy-done.5
  12.9 0.0 copy-done.7
  12.9 0.0 copy-start.1
  13.0 0.7 pair.1
  13.6 1.3 %collective-permute-start.2 = (bf16[256,512]{1,0:T(8,128)(2,1)S(1)}, bf16[256,512]{1,0:T(8,128)(2,1)S(1)}, u32[]{:S(2)}, u32[]{:S(2)}) collective-permute-start(bf16[256,512]{1,0:T(8,128)(2,1)S(1)} %get-tuple-element.17), channel_id=1, source_target_pairs={{0,1},{1,2},{2,3},{3,4},{4,5},{5,6},{6,7},{7,8},{8,9},{9,10},{10,1... | collective-permute-start | bytes 786440 | tf_op jit(solution)/shard_map/ppermute | solution.py:43
  14.9 3.4 %collective-permute-start = (bf16[128,512]{1,0:T(8,128)(2,1)}, bf16[128,512]{1,0:T(8,128)(2,1)}, u32[]{:S(2)}, u32[]{:S(2)}) collective-permute-start(bf16[128,512]{1,0:T(8,128)(2,1)} %get-tuple-element.16), channel_id=1, source_target_pairs={{0,2},{1,3},{2,4},{3,1},{4,6},{5,7},{6,8},{7,5},{8,10},{9,11},{10,... | collective-permute-start | bytes 393224 | tf_op jit(solution)/shard_map/ppermute | solution.py:43
  18.3 3.2 %collective-permute-done.2.near_hbm = bf16[256,512]{1,0:T(8,128)(2,1)S(1)} collective-permute-done((bf16[256,512]{1,0:T(8,128)(2,1)S(1)}, bf16[256,512]{1,0:T(8,128)(2,1)S(1)}, u32[]{:S(2)}, u32[]{:S(2)}) %collective-permute-start.2) | collective-permute-done | bytes 262176 | tf_op jit(solution)/shard_map/ppermute | solution.py:43
  21.5 1.3 %collective-permute-start.3 = (bf16[256,512]{1,0:T(8,128)(2,1)S(1)}, bf16[256,512]{1,0:T(8,128)(2,1)}, u32[]{:S(2)}, u32[]{:S(2)}) collective-permute-start(bf16[256,512]{1,0:T(8,128)(2,1)S(1)} %collective-permute-done.2.near_hbm), channel_id=1, source_target_pairs={{124,64},{64,68},{68,72},{72,76},{76,80},{80,84},{84,88},{88,92},{... | collective-permute-start | bytes 786440 | tf_op jit(solution)/shard_map/ppermute | solution.py:44
  22.8 1.6 %collective-permute-done.far_hbm = bf16[128,512]{1,0:T(8,128)(2,1)} collective-permute-done((bf16[128,512]{1,0:T(8,128)(2,1)}, bf16[128,512]{1,0:T(8,128)(2,1)}, u32[]{:S(2)}, u32[]{:S(2)}) %collective-permute-start) | collective-permute-done | bytes 131104 | tf_op jit(solution)/shard_map/ppermute | solution.py:43
  24.4 1.3 %collective-permute-start.1 = (bf16[128,512]{1,0:T(8,128)(2,1)}, bf16[128,512]{1,0:T(8,128)(2,1)}, u32[]{:S(2)}, u32[]{:S(2)}) collective-permute-start(bf16[128,512]{1,0:T(8,128)(2,1)} %collective-permute-done.far_hbm), channel_id=1, source_target_pairs={{1,5},{5,9},{9,13},{13,17},{17,21},{21,25},{25,29},{29,33},{33,37}... | collective-permute-start | bytes 393224 | tf_op jit(solution)/shard_map/ppermute | solution.py:44
  25.7 0.0 copy-done
  25.8 0.1 pad_add_fusion.place_ref
  25.9 25.4 %collective-permute-done.1.far_fixed = bf16[128,512]{1,0:T(8,128)(2,1)} collective-permute-done((bf16[128,512]{1,0:T(8,128)(2,1)}, bf16[128,512]{1,0:T(8,128)(2,1)}, u32[]{:S(2)}, u32[]{:S(2)}) %collective-permute-start.1) | collective-permute-done | bytes 131104 | tf_op jit(solution)/shard_map/ppermute | solution.py:44
  51.3 0.0 collective-permute-done.3.near_fixed
  51.3 0.0 all-to-all-done.packed_hbm
  51.3 0.0 copy-done.2
  51.3 0.0 copy-done.1
  51.3 0.0 copy-start.6
  51.3 0.0 copy-start.8
  51.3 4.7 %halo_grads.1 = (bf16[128,512]{1,0:T(8,128)(2,1)S(1)}, bf16[256,512]{1,0:T(8,128)(2,1)S(1)}, bf16[192,512]{1,0:T(8,128)(2,1)S(1)}, bf16[192,2048]{1,0:T(8,128)(2,1)S(1)}, bf16[128,2048]{1,0:T(8,128)(2,1)S(1)}) custom-call(s32[3]{0:T(128)S(1)} %pad_add_fusion.place_ref, s32[1,128]{1,0:T(1,128)S(1)} %constant_dynamic-slice_fusion.start_ref, ...), custom_call_target="tpu_custom_call" | custom-call | flops 805306368 | bytes 4194304 | tf_op jit(solution)/shard_map/halo_grads/pallas_call | solution.py:246
  56.0 3.9 %collective-permute-start.4 = (bf16[256,512]{1,0:T(8,128)(2,1)S(1)}, bf16[256,512]{1,0:T(8,128)(2,1)}, u32[]{:S(2)}, u32[]{:S(2)}) collective-permute-start(bf16[256,512]{1,0:T(8,128)(2,1)S(1)} %get-tuple-element.22), channel_id=1, source_target_pairs={{1,0},{2,1},{3,2},{4,3},{5,4},{6,5},{7,6},{8,7},{9,8},{10,9},{11,1... | collective-permute-start | bytes 786440 | tf_op jit(solution)/shard_map/ppermute | solution.py:295
  59.8 3.7 %collective-permute-start.5 = (bf16[128,512]{1,0:T(8,128)(2,1)S(1)}, bf16[128,512]{1,0:T(8,128)(2,1)S(1)}, u32[]{:S(2)}, u32[]{:S(2)}) collective-permute-start(bf16[128,512]{1,0:T(8,128)(2,1)S(1)} %get-tuple-element.23), channel_id=1, source_target_pairs={{2,0},{3,1},{4,2},{5,3},{6,4},{7,5},{8,6},{9,7},{10,8},{11,9},{12,... | collective-permute-start | bytes 393224 | tf_op jit(solution)/shard_map/ppermute | solution.py:19
  63.6 0.0 copy-done.6
  63.6 0.0 copy-done.8
  63.6 7.3 %own_grads.1 = (f32[128,512]{1,0:T(8,128)S(1)}, f32[128,512]{1,0:T(8,128)S(1)}, bf16[128,4096]{1,0:T(8,128)(2,1)}) custom-call(s32[3]{0:T(128)S(1)} %pad_add_fusion.place_ref, s32[1,128]{1,0:T(1,128)S(1)} %constant_dynamic-slice_fusion.start_ref, bf16[128,4096]{1,0:T(8,128)(2,1)S(1)} %copy-done.1, bf16[128,4096]{1,0:T(8,128)(2,1)S(1)} %copy-done.2, ...), custom_call_target="tpu_custom_call" | custom-call | flops 805306368 | bytes 4194304 | tf_op jit(solution)/shard_map/own_grads/pallas_call | solution.py:246
  70.9 0.0 copy-start.3
  70.9 0.7 copy-done.3
  71.6 5.8 %collective-permute-done.5 = bf16[128,512]{1,0:T(8,128)(2,1)S(1)} collective-permute-done((bf16[128,512]{1,0:T(8,128)(2,1)S(1)}, bf16[128,512]{1,0:T(8,128)(2,1)S(1)}, u32[]{:S(2)}, u32[]{:S(2)}) %collective-permute-start.5) | collective-permute-done | bytes 131104 | tf_op jit(solution)/shard_map/ppermute | solution.py:19
  77.4 0.0 copy-start.9
  77.4 0.0 copy-start.4
  77.4 0.0 collective-permute-done.4
  77.4 0.6 copy-done.9
  78.0 0.7 collective-permute-start.6
  78.7 0.9 %fusion = (f32[64,512]{1,0:T(8,128)S(1)}, f32[64,512]{1,0:T(8,128)S(1)}) fusion(bf16[128,512]{1,0:T(8,128)(2,1)} %copy-done.9), kind=kLoop, calls=%fused_computation.5 | loop fusion | bytes 524288 | tf_op jit(solution)/shard_map/slice | solution.py:308
  79.6 0.0 collective-permute-done.6
  79.6 1.0 %select_select_fusion = bf16[256,512]{1,0:T(8,128)(2,1)S(1)} fusion(bf16[256,512]{1,0:T(8,128)(2,1)S(1)} %collective-permute-done.6, bf16[256,512]{1,0:T(8,128)(2,1)} %collective-permute-done.4, pred[]{:T(512)S(6)} %eq.27, pred[]{:T(512)S(6)} %eq.26), kind=kLoop, calls=%fused_computation.2 | loop fusion | flops 262144 | bytes 786434 | tf_op jit(solution)/shard_map/jit(_where)/select_n | solution.py:302
  80.6 0.0 copy-done.4
  80.6 0.8 add_convert_fusion
  (1 shorter events, 0.0 us)
Async XLA Ops:
  0.6 25.1 %copy-start = (s32[8,128]{1,0:T(8,128)S(1)}, s32[8,128]{1,0:T(8,128)}, u32[]{:S(2)}) copy-start(s32[8,128]{1,0:T(8,128)} %param.13) | copy-start | bytes 12292
  3.7 9.3 %copy-start.5 = (bf16[128,512]{1,0:T(8,128)(2,1)S(1)}, bf16[128,512]{1,0:T(8,128)(2,1)}, u32[]{:S(2)}) copy-start(bf16[128,512]{1,0:T(8,128)(2,1)} %k_own.1) | copy-start | bytes 393220
  3.7 9.3 %copy-start.7 = (bf16[128,512]{1,0:T(8,128)(2,1)S(1)}, bf16[128,512]{1,0:T(8,128)(2,1)}, u32[]{:S(2)}) copy-start(bf16[128,512]{1,0:T(8,128)(2,1)} %v_own.1) | copy-start | bytes 393220
  3.7 47.6 %copy-start.2 = (bf16[128,4096]{1,0:T(8,128)(2,1)S(1)}, bf16[128,4096]{1,0:T(8,128)(2,1)}, u32[]{:S(2)}) copy-start(bf16[128,4096]{1,0:T(8,128)(2,1)} %g_ref.3) | copy-start | bytes 3145732
  3.7 47.6 %all-to-all-start = ((bf16[8,144,512]{2,1,0:T(8,128)(2,1)}), bf16[8,144,512]{2,1,0:T(8,128)(2,1)S(1)}, u32[]{:S(2)}, u32[]{:S(2)}) async-start(bf16[8,144,512]{2,1,0:T(8,128)(2,1)} %pack.1), calls=%async_computation | async-start | bytes 2359296 | tf_op jit(solution)/shard_map/all_to_all | solution.py:282
  12.9 38.3 %copy-start.1 = (bf16[128,4096]{1,0:T(8,128)(2,1)S(1)}, bf16[128,4096]{1,0:T(8,128)(2,1)}, u32[]{:S(2)}) copy-start(bf16[128,4096]{1,0:T(8,128)(2,1)} %q_ref.3) | copy-start | bytes 3145732
  13.6 7.9 %collective-permute-start.2 = (bf16[256,512]{1,0:T(8,128)(2,1)S(1)}, bf16[256,512]{1,0:T(8,128)(2,1)S(1)}, u32[]{:S(2)}, u32[]{:S(2)}) collective-permute-start(bf16[256,512]{1,0:T(8,128)(2,1)S(1)} %get-tuple-element.17), channel_id=1, source_target_pairs={{0,1},{1,2},{2,3},{3,4},{4,5},{5,6},{6,7},{7,8},{8,9},{9,10},{10,1... | collective-permute-start | bytes 786440 | tf_op jit(solution)/shard_map/ppermute | solution.py:43
  14.9 9.5 %collective-permute-start = (bf16[128,512]{1,0:T(8,128)(2,1)}, bf16[128,512]{1,0:T(8,128)(2,1)}, u32[]{:S(2)}, u32[]{:S(2)}) collective-permute-start(bf16[128,512]{1,0:T(8,128)(2,1)} %get-tuple-element.16), channel_id=1, source_target_pairs={{0,2},{1,3},{2,4},{3,1},{4,6},{5,7},{6,8},{7,5},{8,10},{9,11},{10,... | collective-permute-start | bytes 393224 | tf_op jit(solution)/shard_map/ppermute | solution.py:43
  21.5 29.7 %collective-permute-start.3 = (bf16[256,512]{1,0:T(8,128)(2,1)S(1)}, bf16[256,512]{1,0:T(8,128)(2,1)}, u32[]{:S(2)}, u32[]{:S(2)}) collective-permute-start(bf16[256,512]{1,0:T(8,128)(2,1)S(1)} %collective-permute-done.2.near_hbm), channel_id=1, source_target_pairs={{124,64},{64,68},{68,72},{72,76},{76,80},{80,84},{84,88},{88,92},{... | collective-permute-start | bytes 786440 | tf_op jit(solution)/shard_map/ppermute | solution.py:44
  24.4 26.8 %collective-permute-start.1 = (bf16[128,512]{1,0:T(8,128)(2,1)}, bf16[128,512]{1,0:T(8,128)(2,1)}, u32[]{:S(2)}, u32[]{:S(2)}) collective-permute-start(bf16[128,512]{1,0:T(8,128)(2,1)} %collective-permute-done.far_hbm), channel_id=1, source_target_pairs={{1,5},{5,9},{9,13},{13,17},{17,21},{21,25},{25,29},{29,33},{33,37}... | collective-permute-start | bytes 393224 | tf_op jit(solution)/shard_map/ppermute | solution.py:44
  51.3 12.3 %copy-start.6 = (bf16[128,512]{1,0:T(8,128)(2,1)S(1)}, bf16[128,512]{1,0:T(8,128)(2,1)}, u32[]{:S(2)}) copy-start(bf16[128,512]{1,0:T(8,128)(2,1)} %k_own.1) | copy-start | bytes 393220
  51.3 12.3 %copy-start.8 = (bf16[128,512]{1,0:T(8,128)(2,1)S(1)}, bf16[128,512]{1,0:T(8,128)(2,1)}, u32[]{:S(2)}) copy-start(bf16[128,512]{1,0:T(8,128)(2,1)} %v_own.1) | copy-start | bytes 393220
  56.0 21.4 %collective-permute-start.4 = (bf16[256,512]{1,0:T(8,128)(2,1)S(1)}, bf16[256,512]{1,0:T(8,128)(2,1)}, u32[]{:S(2)}, u32[]{:S(2)}) collective-permute-start(bf16[256,512]{1,0:T(8,128)(2,1)S(1)} %get-tuple-element.22), channel_id=1, source_target_pairs={{1,0},{2,1},{3,2},{4,3},{5,4},{6,5},{7,6},{8,7},{9,8},{10,9},{11,1... | collective-permute-start | bytes 786440 | tf_op jit(solution)/shard_map/ppermute | solution.py:295
  59.8 17.5 %collective-permute-start.5 = (bf16[128,512]{1,0:T(8,128)(2,1)S(1)}, bf16[128,512]{1,0:T(8,128)(2,1)S(1)}, u32[]{:S(2)}, u32[]{:S(2)}) collective-permute-start(bf16[128,512]{1,0:T(8,128)(2,1)S(1)} %get-tuple-element.23), channel_id=1, source_target_pairs={{2,0},{3,1},{4,2},{5,3},{6,4},{7,5},{8,6},{9,7},{10,8},{11,9},{12,... | collective-permute-start | bytes 393224 | tf_op jit(solution)/shard_map/ppermute | solution.py:19
  70.9 0.7 copy-start.3
  77.4 0.7 copy-start.9
  77.4 3.2 %copy-start.4 = (f32[128,512]{1,0:T(8,128)S(1)}, f32[128,512]{1,0:T(8,128)}, u32[]{:S(2)}) copy-start(f32[128,512]{1,0:T(8,128)} %copy-done.3) | copy-start | bytes 786436
  78.0 1.6 %collective-permute-start.6 = (bf16[256,512]{1,0:T(8,128)(2,1)}, bf16[256,512]{1,0:T(8,128)(2,1)S(1)}, u32[]{:S(2)}, u32[]{:S(2)}) collective-permute-start(bf16[256,512]{1,0:T(8,128)(2,1)} %collective-permute-done.4), channel_id=1, source_target_pairs={{511,383}} | collective-permute-start | bytes 786440 | tf_op jit(solution)/shard_map/ppermute | solution.py:301

commit v5 on v4

--- a/solution.py
+++ b/solution.py
@@ -299,13 +299,15 @@
         scratch=packed_scratch)
     r_near, r_far, dk_own = lax.optimization_barrier((r_near, r_far, dk_own))
     relayed = lax.ppermute(r_near, AXES, [(count - 1, slow - 1)])
-    r_near = jnp.where(index == slow - 1, relayed, jnp.where(index == count - 1, jnp.zeros_like(r_near), r_near))
+    direct, through = (index != slow - 1) & (index != count - 1), index == slow - 1
     r_far = r_far.astype(f32)
 
-    def total(own, near_part, far_part):
-        return (own + near_part.astype(f32) + jnp.pad(far_part, ((half, 0), (0, 0)))).astype(bf16)
-
-    return (grad_queries, total(dk_own, r_near[:tokens], r_far[:half]), total(dv_own, r_near[tokens:], r_far[half:]))
+    def total(own, part, far_part):
+        near_part = jnp.where(direct, r_near[part].astype(f32), 0.0)
+        near_part = jnp.where(through, relayed[part].astype(f32), near_part)
+        return (own + near_part + jnp.pad(far_part, ((half, 0), (0, 0)))).astype(bf16)
+
+    return (grad_queries, total(dk_own, slice(0, tokens), r_far[:half]), total(dv_own, slice(tokens, 2 * tokens), r_far[half:]))
 
 
 def solution(mesh):

time: 81.9 us -> 82 us (level)
    convert_element_type x1, other arithmetic: 0.8 us -> 1.88 us  [total(): (own + near_part + jnp.pad(far_part, ((half, 0), (0, 0)))).astype(bf16)]
    select_n x1 -> x0, other arithmetic: 0.99 us -> none  [body(): jnp.where(index == slow - 1, relayed, jnp.where(index == count - 1, jnp.z...]
where the time goes in v5:
time: 82 us; the launch traced here: 81.5 us
  waiting for transfers between devices  36 us (44%)
  starting transfers between devices  24.7 us (30%)
  Pallas kernels  15.7 us (19%)
  local copies, waits for them, and re-layouts  2.29 us (3%)
  other arithmetic  1.96 us (2%)
  between operations  0.89 us (1%)
    ppermute x2, waiting for transfers between devices, passed_on(): return (arrived, lax.ppermute(arrived, AXES, across))  25.4 us
    pallas_call x4, Pallas kernels, call(): pl.pallas_call(kernel, in_specs=[smem if a.ndim == 1 else vmem for a in a...  15.7 us
    all_to_all x1, starting transfers between devices, body(): lax.all_to_all(packed, 'ulysses', split_axis=0, concat_axis=0, tiled=True)  9.24 us
    ppermute x1, waiting for transfers between devices, shifted(): return lax.ppermute(value, AXES, pairs)  5.77 us
    ppermute x2, waiting for transfers between devices, passed_on(): arrived = lax.ppermute(value, AXES, direct)  4.81 us
    ppermute x2, starting transfers between devices, passed_on(): arrived = lax.ppermute(value, AXES, direct)  4.68 us
    ppermute x1, starting transfers between devices, body(): r_near = lax.ppermute(r_near, AXES, back)  3.85 us
    ppermute x1, starting transfers between devices, shifted(): return lax.ppermute(value, AXES, pairs)  3.73 us
  transfers between devices with their start and end apart: 8, of which 4 were waited for; matrix products, arithmetic and copies ran while one was open for 1% of the time, Pallas kernels for 10%

profile of v5, /device:TPU:24, one launch (start us, length us, event | category | flops | bytes accessed | tf_op | source)
XLA Modules:
  0.0 81.5 jit_solution(3799342794261090618)
XLA Ops:
  0.6 0.0 copy-start
  0.6 3.0 %pack.1 = bf16[8,144,512]{2,1,0:T(8,128)(2,1)} custom-call(f32[8,4,128]{2,1,0:T(4,128)} %log_ref.1, bf16[8,128,512]{2,1,0:T(8,128)(2,1)} %o_hbm.1), custom_call_target="tpu_custom_call" | custom-call | bytes 4194304 | tf_op jit(solution)/shard_map/pack/pallas_call | solution.py:246
  3.7 0.0 copy-start.4
  3.7 0.0 copy-start.6
  3.7 0.0 copy-start.2
  3.7 9.2 %all-to-all-start = ((bf16[8,144,512]{2,1,0:T(8,128)(2,1)}), bf16[8,144,512]{2,1,0:T(8,128)(2,1)S(1)}, u32[]{:S(2)}, u32[]{:S(2)}) async-start(bf16[8,144,512]{2,1,0:T(8,128)(2,1)} %pack.1), calls=%async_computation | async-start | bytes 2359296 | tf_op jit(solution)/shard_map/all_to_all | solution.py:282
  12.9 0.0 copy-done.4
  12.9 0.0 copy-done.6
  12.9 0.0 copy-start.1
  13.0 0.7 pair.1
  13.6 1.3 %collective-permute-start.2 = (bf16[256,512]{1,0:T(8,128)(2,1)S(1)}, bf16[256,512]{1,0:T(8,128)(2,1)S(1)}, u32[]{:S(2)}, u32[]{:S(2)}) collective-permute-start(bf16[256,512]{1,0:T(8,128)(2,1)S(1)} %get-tuple-element.17), channel_id=1, source_target_pairs={{0,1},{1,2},{2,3},{3,4},{4,5},{5,6},{6,7},{7,8},{8,9},{9,10},{10,1... | collective-permute-start | bytes 786440 | tf_op jit(solution)/shard_map/ppermute | solution.py:43
  14.9 3.4 %collective-permute-start = (bf16[128,512]{1,0:T(8,128)(2,1)}, bf16[128,512]{1,0:T(8,128)(2,1)}, u32[]{:S(2)}, u32[]{:S(2)}) collective-permute-start(bf16[128,512]{1,0:T(8,128)(2,1)} %get-tuple-element.16), channel_id=1, source_target_pairs={{0,2},{1,3},{2,4},{3,1},{4,6},{5,7},{6,8},{7,5},{8,10},{9,11},{10,... | collective-permute-start | bytes 393224 | tf_op jit(solution)/shard_map/ppermute | solution.py:43
  18.3 3.2 %collective-permute-done.2.near_hbm = bf16[256,512]{1,0:T(8,128)(2,1)S(1)} collective-permute-done((bf16[256,512]{1,0:T(8,128)(2,1)S(1)}, bf16[256,512]{1,0:T(8,128)(2,1)S(1)}, u32[]{:S(2)}, u32[]{:S(2)}) %collective-permute-start.2) | collective-permute-done | bytes 262176 | tf_op jit(solution)/shard_map/ppermute | solution.py:43
  21.5 1.3 %collective-permute-start.3 = (bf16[256,512]{1,0:T(8,128)(2,1)S(1)}, bf16[256,512]{1,0:T(8,128)(2,1)}, u32[]{:S(2)}, u32[]{:S(2)}) collective-permute-start(bf16[256,512]{1,0:T(8,128)(2,1)S(1)} %collective-permute-done.2.near_hbm), channel_id=1, source_target_pairs={{124,64},{64,68},{68,72},{72,76},{76,80},{80,84},{84,88},{88,92},{... | collective-permute-start | bytes 786440 | tf_op jit(solution)/shard_map/ppermute | solution.py:44
  22.8 1.6 %collective-permute-done.far_hbm = bf16[128,512]{1,0:T(8,128)(2,1)} collective-permute-done((bf16[128,512]{1,0:T(8,128)(2,1)}, bf16[128,512]{1,0:T(8,128)(2,1)}, u32[]{:S(2)}, u32[]{:S(2)}) %collective-permute-start) | collective-permute-done | bytes 131104 | tf_op jit(solution)/shard_map/ppermute | solution.py:43
  24.4 1.3 %collective-permute-start.1 = (bf16[128,512]{1,0:T(8,128)(2,1)}, bf16[128,512]{1,0:T(8,128)(2,1)}, u32[]{:S(2)}, u32[]{:S(2)}) collective-permute-start(bf16[128,512]{1,0:T(8,128)(2,1)} %collective-permute-done.far_hbm), channel_id=1, source_target_pairs={{1,5},{5,9},{9,13},{13,17},{17,21},{21,25},{25,29},{29,33},{33,37}... | collective-permute-start | bytes 393224 | tf_op jit(solution)/shard_map/ppermute | solution.py:44
  25.7 0.0 copy-done
  25.8 0.1 pad_add_fusion.place_ref
  25.9 25.4 %collective-permute-done.1.far_fixed = bf16[128,512]{1,0:T(8,128)(2,1)} collective-permute-done((bf16[128,512]{1,0:T(8,128)(2,1)}, bf16[128,512]{1,0:T(8,128)(2,1)}, u32[]{:S(2)}, u32[]{:S(2)}) %collective-permute-start.1) | collective-permute-done | bytes 131104 | tf_op jit(solution)/shard_map/ppermute | solution.py:44
  51.3 0.0 collective-permute-done.3.near_fixed
  51.3 0.0 all-to-all-done.packed_hbm
  51.3 0.0 copy-done.2
  51.3 0.0 copy-done.1
  51.3 0.0 copy-start.5
  51.3 0.0 copy-start.7
  51.3 4.7 %halo_grads.1 = (bf16[128,512]{1,0:T(8,128)(2,1)S(1)}, bf16[256,512]{1,0:T(8,128)(2,1)S(1)}, bf16[192,512]{1,0:T(8,128)(2,1)S(1)}, bf16[192,2048]{1,0:T(8,128)(2,1)S(1)}, bf16[128,2048]{1,0:T(8,128)(2,1)S(1)}) custom-call(s32[3]{0:T(128)S(1)} %pad_add_fusion.place_ref, s32[1,128]{1,0:T(1,128)S(1)} %constant_dynamic-slice_fusion.start_ref, ...), custom_call_target="tpu_custom_call" | custom-call | flops 805306368 | bytes 4194304 | tf_op jit(solution)/shard_map/halo_grads/pallas_call | solution.py:246
  56.0 3.9 %collective-permute-start.4 = (bf16[256,512]{1,0:T(8,128)(2,1)S(1)}, bf16[256,512]{1,0:T(8,128)(2,1)}, u32[]{:S(2)}, u32[]{:S(2)}) collective-permute-start(bf16[256,512]{1,0:T(8,128)(2,1)S(1)} %get-tuple-element.22), channel_id=1, source_target_pairs={{1,0},{2,1},{3,2},{4,3},{5,4},{6,5},{7,6},{8,7},{9,8},{10,9},{11,1... | collective-permute-start | bytes 786440 | tf_op jit(solution)/shard_map/ppermute | solution.py:295
  59.8 3.7 %collective-permute-start.5 = (bf16[128,512]{1,0:T(8,128)(2,1)S(1)}, bf16[128,512]{1,0:T(8,128)(2,1)S(1)}, u32[]{:S(2)}, u32[]{:S(2)}) collective-permute-start(bf16[128,512]{1,0:T(8,128)(2,1)S(1)} %get-tuple-element.23), channel_id=1, source_target_pairs={{2,0},{3,1},{4,2},{5,3},{6,4},{7,5},{8,6},{9,7},{10,8},{11,9},{12,... | collective-permute-start | bytes 393224 | tf_op jit(solution)/shard_map/ppermute | solution.py:19
  63.6 0.0 copy-done.5
  63.6 0.0 copy-done.7
  63.6 7.3 %own_grads.1 = (f32[128,512]{1,0:T(8,128)S(1)}, f32[128,512]{1,0:T(8,128)S(1)}, bf16[128,4096]{1,0:T(8,128)(2,1)}) custom-call(s32[3]{0:T(128)S(1)} %pad_add_fusion.place_ref, s32[1,128]{1,0:T(1,128)S(1)} %constant_dynamic-slice_fusion.start_ref, bf16[128,4096]{1,0:T(8,128)(2,1)S(1)} %copy-done.1, bf16[128,4096]{1,0:T(8,128)(2,1)S(1)} %copy-done.2, ...), custom_call_target="tpu_custom_call" | custom-call | flops 805306368 | bytes 4194304 | tf_op jit(solution)/shard_map/own_grads/pallas_call | solution.py:246
  70.9 0.0 copy-start.3
  70.9 0.7 copy-done.3
  71.6 5.8 %collective-permute-done.5 = bf16[128,512]{1,0:T(8,128)(2,1)S(1)} collective-permute-done((bf16[128,512]{1,0:T(8,128)(2,1)S(1)}, bf16[128,512]{1,0:T(8,128)(2,1)S(1)}, u32[]{:S(2)}, u32[]{:S(2)}) %collective-permute-start.5) | collective-permute-done | bytes 131104 | tf_op jit(solution)/shard_map/ppermute | solution.py:19
  77.4 0.0 copy-start.8
  77.4 0.0 collective-permute-done.4
  77.4 0.6 copy-done.8
  78.0 0.7 collective-permute-start.6
  78.7 0.9 %fusion = (f32[64,512]{1,0:T(8,128)S(1)}, f32[64,512]{1,0:T(8,128)S(1)}) fusion(bf16[128,512]{1,0:T(8,128)(2,1)} %copy-done.8), kind=kLoop, calls=%fused_computation.4 | loop fusion | bytes 524288 | tf_op jit(solution)/shard_map/slice | solution.py:310
  79.6 0.0 collective-permute-done.6
  79.6 1.9 %add_convert_fusion = (bf16[128,512]{1,0:T(8,128)(2,1)}, bf16[128,512]{1,0:T(8,128)(2,1)}) fusion(f32[64,512]{1,0:T(8,128)S(1)} %get-tuple-element.31, f32[128,512]{1,0:T(8,128)} %copy-done.3, bf16[256,512]{1,0:T(8,128)(2,1)S(1)} %collective-permute-done.6, bf16[256,512]{1,0:T(8,128)(2,1)} %collective-permute-done.4, pred[]{:T(512)S(6)} %and.20, pred[]{:T(512)S(6)} %eq.23, ...), kind=kLoop, calls=%fused_computation | loop fusion | flops 917504 | bytes 1572866 | tf_op jit(solution)/shard_map/convert_element_type | solution.py:308
  (1 shorter events, 0.0 us)
Async XLA Ops:
  0.6 25.1 %copy-start = (s32[8,128]{1,0:T(8,128)S(1)}, s32[8,128]{1,0:T(8,128)}, u32[]{:S(2)}) copy-start(s32[8,128]{1,0:T(8,128)} %param.13) | copy-start | bytes 12292
  3.7 9.3 %copy-start.4 = (bf16[128,512]{1,0:T(8,128)(2,1)S(1)}, bf16[128,512]{1,0:T(8,128)(2,1)}, u32[]{:S(2)}) copy-start(bf16[128,512]{1,0:T(8,128)(2,1)} %k_own.1) | copy-start | bytes 393220
  3.7 9.3 %copy-start.6 = (bf16[128,512]{1,0:T(8,128)(2,1)S(1)}, bf16[128,512]{1,0:T(8,128)(2,1)}, u32[]{:S(2)}) copy-start(bf16[128,512]{1,0:T(8,128)(2,1)} %v_own.1) | copy-start | bytes 393220
  3.7 47.6 %copy-start.2 = (bf16[128,4096]{1,0:T(8,128)(2,1)S(1)}, bf16[128,4096]{1,0:T(8,128)(2,1)}, u32[]{:S(2)}) copy-start(bf16[128,4096]{1,0:T(8,128)(2,1)} %g_ref.3) | copy-start | bytes 3145732
  3.7 47.6 %all-to-all-start = ((bf16[8,144,512]{2,1,0:T(8,128)(2,1)}), bf16[8,144,512]{2,1,0:T(8,128)(2,1)S(1)}, u32[]{:S(2)}, u32[]{:S(2)}) async-start(bf16[8,144,512]{2,1,0:T(8,128)(2,1)} %pack.1), calls=%async_computation | async-start | bytes 2359296 | tf_op jit(solution)/shard_map/all_to_all | solution.py:282
  12.9 38.3 %copy-start.1 = (bf16[128,4096]{1,0:T(8,128)(2,1)S(1)}, bf16[128,4096]{1,0:T(8,128)(2,1)}, u32[]{:S(2)}) copy-start(bf16[128,4096]{1,0:T(8,128)(2,1)} %q_ref.3) | copy-start | bytes 3145732
  13.6 7.9 %collective-permute-start.2 = (bf16[256,512]{1,0:T(8,128)(2,1)S(1)}, bf16[256,512]{1,0:T(8,128)(2,1)S(1)}, u32[]{:S(2)}, u32[]{:S(2)}) collective-permute-start(bf16[256,512]{1,0:T(8,128)(2,1)S(1)} %get-tuple-element.17), channel_id=1, source_target_pairs={{0,1},{1,2},{2,3},{3,4},{4,5},{5,6},{6,7},{7,8},{8,9},{9,10},{10,1... | collective-permute-start | bytes 786440 | tf_op jit(solution)/shard_map/ppermute | solution.py:43
  14.9 9.5 %collective-permute-start = (bf16[128,512]{1,0:T(8,128)(2,1)}, bf16[128,512]{1,0:T(8,128)(2,1)}, u32[]{:S(2)}, u32[]{:S(2)}) collective-permute-start(bf16[128,512]{1,0:T(8,128)(2,1)} %get-tuple-element.16), channel_id=1, source_target_pairs={{0,2},{1,3},{2,4},{3,1},{4,6},{5,7},{6,8},{7,5},{8,10},{9,11},{10,... | collective-permute-start | bytes 393224 | tf_op jit(solution)/shard_map/ppermute | solution.py:43
  21.5 29.7 %collective-permute-start.3 = (bf16[256,512]{1,0:T(8,128)(2,1)S(1)}, bf16[256,512]{1,0:T(8,128)(2,1)}, u32[]{:S(2)}, u32[]{:S(2)}) collective-permute-start(bf16[256,512]{1,0:T(8,128)(2,1)S(1)} %collective-permute-done.2.near_hbm), channel_id=1, source_target_pairs={{124,64},{64,68},{68,72},{72,76},{76,80},{80,84},{84,88},{88,92},{... | collective-permute-start | bytes 786440 | tf_op jit(solution)/shard_map/ppermute | solution.py:44
  24.4 26.8 %collective-permute-start.1 = (bf16[128,512]{1,0:T(8,128)(2,1)}, bf16[128,512]{1,0:T(8,128)(2,1)}, u32[]{:S(2)}, u32[]{:S(2)}) collective-permute-start(bf16[128,512]{1,0:T(8,128)(2,1)} %collective-permute-done.far_hbm), channel_id=1, source_target_pairs={{1,5},{5,9},{9,13},{13,17},{17,21},{21,25},{25,29},{29,33},{33,37}... | collective-permute-start | bytes 393224 | tf_op jit(solution)/shard_map/ppermute | solution.py:44
  51.3 12.3 %copy-start.5 = (bf16[128,512]{1,0:T(8,128)(2,1)S(1)}, bf16[128,512]{1,0:T(8,128)(2,1)}, u32[]{:S(2)}) copy-start(bf16[128,512]{1,0:T(8,128)(2,1)} %k_own.1) | copy-start | bytes 393220
  51.3 12.3 %copy-start.7 = (bf16[128,512]{1,0:T(8,128)(2,1)S(1)}, bf16[128,512]{1,0:T(8,128)(2,1)}, u32[]{:S(2)}) copy-start(bf16[128,512]{1,0:T(8,128)(2,1)} %v_own.1) | copy-start | bytes 393220
  56.0 21.4 %collective-permute-start.4 = (bf16[256,512]{1,0:T(8,128)(2,1)S(1)}, bf16[256,512]{1,0:T(8,128)(2,1)}, u32[]{:S(2)}, u32[]{:S(2)}) collective-permute-start(bf16[256,512]{1,0:T(8,128)(2,1)S(1)} %get-tuple-element.22), channel_id=1, source_target_pairs={{1,0},{2,1},{3,2},{4,3},{5,4},{6,5},{7,6},{8,7},{9,8},{10,9},{11,1... | collective-permute-start | bytes 786440 | tf_op jit(solution)/shard_map/ppermute | solution.py:295
  59.8 17.5 %collective-permute-start.5 = (bf16[128,512]{1,0:T(8,128)(2,1)S(1)}, bf16[128,512]{1,0:T(8,128)(2,1)S(1)}, u32[]{:S(2)}, u32[]{:S(2)}) collective-permute-start(bf16[128,512]{1,0:T(8,128)(2,1)S(1)} %get-tuple-element.23), channel_id=1, source_target_pairs={{2,0},{3,1},{4,2},{5,3},{6,4},{7,5},{8,6},{9,7},{10,8},{11,9},{12,... | collective-permute-start | bytes 393224 | tf_op jit(solution)/shard_map/ppermute | solution.py:19
  70.9 0.7 copy-start.3
  77.4 0.7 copy-start.8
  78.0 1.6 %collective-permute-start.6 = (bf16[256,512]{1,0:T(8,128)(2,1)}, bf16[256,512]{1,0:T(8,128)(2,1)S(1)}, u32[]{:S(2)}, u32[]{:S(2)}) collective-permute-start(bf16[256,512]{1,0:T(8,128)(2,1)} %collective-permute-done.4), channel_id=1, source_target_pairs={{511,383}} | collective-permute-start | bytes 786440 | tf_op jit(solution)/shard_map/ppermute | solution.py:301
